TPU v7x, 256 devices: a whole 4x4x8 slice. The times are simulated.
256 devices in a mesh: ctx: 32 (over z, x_lo, core), head: 8 (over x_hi, y).
Axes of the slice: x: 4 (x_hi: 2, x_lo: 2; x = x_hi * 2 + x_lo), y: 4, z: 8, core: 2. Of those that a mesh axis runs over, the one named last changes fastest.
Arguments:
- kv_latent: bfloat16 [16384, 576], P('ctx'), may hold values from -4 to 4
- queries: bfloat16 [16384, 3072], P('ctx', 'head'), may hold values from -22 to 22
- grad_out: bfloat16 [16384, 2048], P('ctx', 'head'), may hold values from -6 to 6
- kv_up_weight: bfloat16 [512, 4096], P(None, 'head'), may hold values from -0.25 to 0.25
- doc_ids: int32 [16384], replicated, may hold values from 0 to 15, never falling along the last dimension, each value on 1 to 1536 neighbouring positions
Outputs:
- grad_queries: bfloat16 [16384, 3072], P('ctx', 'head')
- grad_latent: bfloat16 [16384, 576], P('ctx')
- grad_weight: float32 [512, 4096], P('ctx', 'head')
Inputs may be any that keep to these rules, and one draw needn't show every extreme that they name: `doc_ids`: document ids never fall along the sequence; every document has 1 to 1536 tokens, and one has exactly 1536.
All inputs are finite; a program needn't handle non-finite values.
Results may differ from a plain program's by a relative error of at most 0.0076.
Values may be sent and summed in bfloat16 or wider, within the bound.
A program may use at most 64 MiB of HBM per device.

v0:
```python
import math

import jax
import jax.numpy as jnp
from jax import lax
from jax.sharding import PartitionSpec as P

NOPE = 128
ROPE = 64
VDIM = 128
LATENT = 512
REACH = 3
KEY_BLOCK = 512


masked_score = -1e30


def from_behind(value, axis, steps):
    count = lax.axis_size(axis)
    initial, last = (max(0, -steps), min(count, count - steps))
    return lax.ppermute(value, axis, [(source, source + steps) for source in range(initial, last)])


def local(kv_latent, queries, grad_out, kv_up_weight, doc_ids):
    row_count = kv_latent.shape[0]
    token_total = doc_ids.shape[0]
    head_count = kv_up_weight.shape[1] // (NOPE + VDIM)
    kv_width = head_count * (NOPE + VDIM)
    score_scale = 1.0 / math.sqrt(NOPE + ROPE)
    first_row = lax.axis_index("ctx") * row_count
    window_rows = (REACH + 1) * row_count
    window_start = first_row - REACH * row_count
    earlier = [kv_latent] + [
        from_behind(kv_latent, "ctx", offset) for offset in range(1, REACH + 1)
    ]
    stacked = jnp.concatenate(earlier[::-1], axis=0)
    lifted = jnp.dot(stacked[:, :LATENT], kv_up_weight, preferred_element_type=jnp.float32)
    key_side = jnp.concatenate([lifted.astype(jnp.bfloat16), stacked[:, LATENT:]], axis=1)
    query_heads = queries.reshape(row_count, head_count, NOPE + ROPE)
    query_nope = query_heads[:, :, :NOPE]
    query_rope = query_heads[:, :, NOPE:]
    out_heads = grad_out.reshape(row_count, head_count, VDIM)
    my_docs = lax.dynamic_slice_in_dim(doc_ids, first_row, row_count)
    query_pos = first_row + jnp.arange(row_count, dtype=jnp.int32)

    def block_parts(block_index):
        block_start = (block_index * KEY_BLOCK).astype(jnp.int32)
        key_rows = lax.dynamic_slice_in_dim(key_side, block_start, KEY_BLOCK, 0)
        pairs = key_rows[:, :kv_width].reshape(KEY_BLOCK, head_count, NOPE + VDIM)
        key_nope = pairs[:, :, :NOPE]
        values = pairs[:, :, NOPE:]
        key_rope = key_rows[:, kv_width:]
        key_pos = window_start + block_start + jnp.arange(KEY_BLOCK, dtype=jnp.int32)
        key_docs = jnp.take(doc_ids, jnp.clip(key_pos, 0, token_total - 1))
        visible = (
            (my_docs[:, None] == key_docs[None, :])
            & (key_pos[None, :] <= query_pos[:, None])
            & (key_pos[None, :] >= 0)
        )
        scores = score_scale * (
            jnp.einsum("thd,khd->htk", query_nope, key_nope, preferred_element_type=jnp.float32)
            + jnp.einsum("thd,kd->htk", query_rope, key_rope, preferred_element_type=jnp.float32)
        )
        scores = jnp.where(visible[None], scores, masked_score)
        grad_probs = jnp.einsum(
            "thd,khd->htk", out_heads, values, preferred_element_type=jnp.float32
        )
        return (key_nope, values, key_rope, visible, scores, grad_probs)

    block_total = window_rows // KEY_BLOCK
    block_first = 0

    def first_pass(block_index, carry):
        row_top, row_mass, row_cross = carry
        parts = block_parts(block_index)
        visible, scores, grad_probs = (parts[3], parts[4], parts[5])
        new_top = jnp.maximum(row_top, jnp.max(scores, axis=2))
        factor = jnp.exp(row_top - new_top)
        weights = jnp.where(visible[None], jnp.exp(scores - new_top[:, :, None]), 0.0)
        return (
            new_top,
            row_mass * factor + jnp.sum(weights, axis=2),
            row_cross * factor + jnp.sum(weights * grad_probs, axis=2),
        )

    stat_shape = (head_count, row_count)
    row_top, row_mass, row_cross = lax.fori_loop(
        block_first,
        block_total,
        first_pass,
        (
            jnp.full(stat_shape, masked_score, jnp.float32),
            jnp.zeros(stat_shape, jnp.float32),
            jnp.zeros(stat_shape, jnp.float32),
        ),
    )
    log_total = row_top + jnp.log(row_mass)
    delta = row_cross / row_mass

    def second_pass(block_index, carry):
        grad_qnope, grad_qrope, key_grads = carry
        key_nope, values, key_rope, visible, scores, grad_probs = block_parts(block_index)
        weights = jnp.where(visible[None], jnp.exp(scores - log_total[:, :, None]), 0.0)
        grad_scores = (weights * (grad_probs - delta[:, :, None])).astype(jnp.bfloat16)
        weights_low = weights.astype(jnp.bfloat16)
        grad_qnope = grad_qnope + score_scale * jnp.einsum(
            "htk,khd->thd", grad_scores, key_nope, preferred_element_type=jnp.float32
        )
        grad_qrope = grad_qrope + score_scale * jnp.einsum(
            "htk,kd->thd", grad_scores, key_rope, preferred_element_type=jnp.float32
        )
        grad_keys = score_scale * jnp.einsum(
            "htk,thd->khd", grad_scores, query_nope, preferred_element_type=jnp.float32
        )
        grad_rope = score_scale * jnp.einsum(
            "htk,thd->kd", grad_scores, query_rope, preferred_element_type=jnp.float32
        )
        grad_values = jnp.einsum(
            "htk,thd->khd", weights_low, out_heads, preferred_element_type=jnp.float32
        )
        block_grad = jnp.concatenate(
            [
                jnp.concatenate([grad_keys, grad_values], axis=2).reshape(KEY_BLOCK, kv_width),
                grad_rope,
            ],
            axis=1,
        )
        key_grads = lax.dynamic_update_slice_in_dim(
            key_grads, block_grad, (block_index * KEY_BLOCK).astype(jnp.int32), 0
        )
        return (grad_qnope, grad_qrope, key_grads)

    grad_qnope, grad_qrope, key_grads = lax.fori_loop(
        block_first,
        block_total,
        second_pass,
        (
            jnp.zeros((row_count, head_count, NOPE), jnp.float32),
            jnp.zeros((row_count, head_count, ROPE), jnp.float32),
            jnp.zeros((window_rows, kv_width + ROPE), jnp.float32),
        ),
    )

    def owner_part(offset):
        return key_grads[(REACH - offset) * row_count : (REACH - offset + 1) * row_count]

    summed = owner_part(0)
    for offset in range(1, REACH + 1):
        summed = summed + from_behind(owner_part(offset), "ctx", -offset)
    kv_grad = summed[:, :kv_width].astype(jnp.bfloat16)
    rope_grad = summed[:, kv_width:]
    latent_part = lax.dot_general(
        kv_grad, kv_up_weight, (((1,), (1,)), ((), ())), preferred_element_type=jnp.float32
    )
    latent_total = lax.psum(jnp.concatenate([latent_part, rope_grad], axis=1), "head")
    latent_cols = lax.slice_in_dim(
        kv_latent, 0, lax.axis_size("ctx") * (LATENT // lax.axis_size("ctx")), axis=1
    )
    grad_weight = lax.psum_scatter(
        lax.dot_general(
            latent_cols, kv_grad, (((0,), (0,)), ((), ())), preferred_element_type=jnp.float32
        ),
        "ctx",
        scatter_dimension=0,
        tiled=True,
    )
    grad_queries = (
        jnp.concatenate([grad_qnope, grad_qrope], axis=2)
        .reshape(row_count, head_count * (NOPE + ROPE))
        .astype(jnp.bfloat16)
    )
    return (grad_queries, latent_total.astype(jnp.bfloat16), grad_weight)


def solution(mesh):
    return jax.shard_map(
        local,
        mesh=mesh,
        in_specs=(P("ctx", None), P("ctx", "head"), P("ctx", "head"), P(None, "head"), P()),
        out_specs=(P("ctx", "head"), P("ctx", None), P("ctx", "head")),
        check_vma=False,
    )
```

profile of v0, /device:TPU:1, one launch (start us, length us, event | category | flops | bytes accessed | tf_op | source)
XLA Modules:
  0.0 330.3 jit_solution(5811115365233028075)
XLA Ops:
  7.2 5.9 %collective-permute-start = (bf16[512,576]{0,1:T(8,128)(2,1)}, bf16[512,576]{0,1:T(8,128)(2,1)}, u32[]{:S(2)}, u32[]{:S(2)}) collective-permute-start(bf16[512,576]{0,1:T(8,128)(2,1)} %param.11), channel_id=1, source_target_pairs={{0,24},{8,32},{16,40},{24,48},{32,56},{40,64},{48,72},{56,80},{64,... | collective-permute-start | bytes 1769480 | tf_op jit(solution)/shard_map/ppermute | solution.py:22
  13.1 3.1 collective-permute-start.1
  16.3 2.3 collective-permute-start.2
  23.2 5.8 %collective-permute-done.1 = bf16[512,576]{0,1:T(8,128)(2,1)} collective-permute-done((bf16[512,576]{0,1:T(8,128)(2,1)}, bf16[512,576]{0,1:T(8,128)(2,1)}, u32[]{:S(2)}, u32[]{:S(2)}) %collective-permute-start.1) | collective-permute-done | bytes 589856 | tf_op jit(solution)/shard_map/ppermute | solution.py:22
  30.1 8.1 %collective-permute-done.2 = bf16[512,576]{0,1:T(8,128)(2,1)S(1)} collective-permute-done((bf16[512,576]{0,1:T(8,128)(2,1)}, bf16[512,576]{0,1:T(8,128)(2,1)S(1)}, u32[]{:S(2)}, u32[]{:S(2)}) %collective-permute-start.2) | collective-permute-done | bytes 589856 | tf_op jit(solution)/shard_map/ppermute | solution.py:22
  41.5 32.1 %while.36 = (s32[]{:T(128)}, f32[2,512]{1,0:T(2,128)S(1)}, f32[2,512]{1,0:T(2,128)S(1)}, f32[2,512]{1,0:T(2,128)S(1)}, s32[512]{0:T(512)S(1)}, /*index=5*/s32[]{...) while((s32[]{:T(128)}, f32[2,512]{1,0:T(2,128)S(1)}, ...), condition=%wide.region_4.6_spmd.clone, body=%wide.region_0.5_spmd.clone.sunk | while | flops 342376960 | bytes 13933842 | solution.py:88
  41.5 3.1 gather_fusion
  49.5 3.1 gather_fusion
  57.5 3.1 gather_fusion
  65.6 3.1 gather_fusion
  73.6 2.7 broadcast_in_dim.131
  76.3 46.1 %while.37 = (s32[]{:T(128)}, f32[512,2,128]{0,2,1:T(8,128)S(1)}, f32[512,2,64]{0,2,1:T(8,128)S(1)}, f32[2048,576]{0,1:T(8,128)}, bf16[2048,576]{0,1:T(8,128)(2,1...) while((s32[]{:T(128)}, f32[512,2,128]{0,2,1:T(8,128)S(1)}, ...), condition=%wide.region_6.8_spmd.clone, body=%wide.region_5.7_spmd.clone.sunk | while | flops 879502848 | bytes 26778924 | solution.py:134
  76.3 3.1 gather_fusion.1
  87.8 3.1 gather_fusion.1
  99.4 3.1 gather_fusion.1
  110.9 3.1 gather_fusion.1
  122.4 2.3 fusion.37
  124.7 1.9 collective-permute-start.3
  129.4 20.3 %collective-permute-done.3 = f32[512,576]{0,1:T(8,128)S(1)} collective-permute-done((f32[512,576]{0,1:T(8,128)S(1)}, f32[512,576]{0,1:T(8,128)S(1)}, u32[]{:S(2)}, u32[]{:S(2)}) %collective-permute-start.3) | collective-permute-done | bytes 1179680 | tf_op jit(solution)/shard_map/ppermute | solution.py:22
  149.7 36.8 %collective-permute-done.5 = f32[512,576]{0,1:T(8,128)S(1)} collective-permute-done((f32[512,576]{0,1:T(8,128)S(1)}, f32[512,576]{0,1:T(8,128)S(1)}, u32[]{:S(2)}, u32[]{:S(2)}) %collective-permute-start.5) | collective-permute-done | bytes 1179680 | tf_op jit(solution)/shard_map/ppermute | solution.py:22
  186.5 1.8 add_add_fusion
  189.8 2.6 copy.66
  194.0 70.0 %all-reduce.1 = bf16[512,576]{0,1:T(8,128)(2,1)} all-reduce(f32[512,576]{0,1:T(8,128)S(1)} %pad_maximum_fusion.2), channel_id=1, replica_groups=mesh['ctx'=32,'head'=8] {'head'}, use_global_device_ids=true, to_apply=%region_7.9 | all-reduce | flops 294912 | bytes 1769472 | tf_op jit(solution)/shard_map/psum | solution.py:156
  263.9 59.5 %reduce-scatter.4.cloned.1.call-done = f32[16,512]{1,0:T(8,128)} async-done(((f32[512,512]{1,0:T(8,128)}), f32[16,512]{1,0:T(8,128)}) %reduce-scatter.4.cloned.1.call-update) | async-done | bytes 32784
  (168 shorter events, 66.9 us)
Async XLA Ops:
  7.2 31.2 %copy-start = (bf16[512,512]{1,0:T(8,128)(2,1)S(1)}, bf16[512,512]{1,0:T(8,128)(2,1)}, u32[]{:S(2)}) copy-start(bf16[512,512]{1,0:T(8,128)(2,1)} %param.14) | copy-start | bytes 1572868
  7.2 14.8 %copy-start.1 = (s32[16384]{0:T(1024)S(1)}, s32[16384]{0:T(1024)}, u32[]{:S(2)}) copy-start(s32[16384]{0:T(1024)} %param.15) | copy-start | bytes 196612
  7.2 316.3 %reduce-scatter.4.cloned.1.call-start = ((), (), s32[]{:S(2)}) async-start(), calls=%async_computation.1 | async-start | bytes 1081344
  7.2 14.8 %collective-permute-start = (bf16[512,576]{0,1:T(8,128)(2,1)}, bf16[512,576]{0,1:T(8,128)(2,1)}, u32[]{:S(2)}, u32[]{:S(2)}) collective-permute-start(bf16[512,576]{0,1:T(8,128)(2,1)} %param.11), channel_id=1, source_target_pairs={{0,24},{8,32},{16,40},{24,48},{32,56},{40,64},{48,72},{56,80},{64,... | collective-permute-start | bytes 1769480 | tf_op jit(solution)/shard_map/ppermute | solution.py:22
  13.1 15.8 %collective-permute-start.1 = (bf16[512,576]{0,1:T(8,128)(2,1)}, bf16[512,576]{0,1:T(8,128)(2,1)}, u32[]{:S(2)}, u32[]{:S(2)}) collective-permute-start(bf16[512,576]{0,1:T(8,128)(2,1)} %param.11), channel_id=1, source_target_pairs={{0,16},{8,24},{16,32},{24,40},{32,48},{40,56},{48,64},{56,72},{64,... | collective-permute-start | bytes 1769480 | tf_op jit(solution)/shard_map/ppermute | solution.py:22
  16.3 21.9 %collective-permute-start.2 = (bf16[512,576]{0,1:T(8,128)(2,1)}, bf16[512,576]{0,1:T(8,128)(2,1)S(1)}, u32[]{:S(2)}, u32[]{:S(2)}) collective-permute-start(bf16[512,576]{0,1:T(8,128)(2,1)} %param.11), channel_id=1, source_target_pairs={{0,8},{8,16},{16,24},{24,32},{32,40},{40,48},{48,56},{56,64},{64,7... | collective-permute-start | bytes 1769480 | tf_op jit(solution)/shard_map/ppermute | solution.py:22
  21.8 16.5 %copy-start.2 = (bf16[512,576]{0,1:T(8,128)(2,1)S(1)}, bf16[512,576]{0,1:T(8,128)(2,1)}, u32[]{:S(2)}) copy-start(bf16[512,576]{0,1:T(8,128)(2,1)} %param.11) | copy-start | bytes 1769476
  39.7 1.7 copy-start.4
  124.7 24.9 %collective-permute-start.3 = (f32[512,576]{0,1:T(8,128)S(1)}, f32[512,576]{0,1:T(8,128)S(1)}, u32[]{:S(2)}, u32[]{:S(2)}) collective-permute-start(f32[512,576]{0,1:T(8,128)S(1)} %get-tuple-element.637), channel_id=1, source_target_pairs={{8,0},{16,8},{24,16},{32,24},{40,32},{48,40},{56,48},{64,56},{72,6... | collective-permute-start | bytes 3538952 | tf_op jit(solution)/shard_map/ppermute | solution.py:22
  126.7 59.8 %collective-permute-start.5 = (f32[512,576]{0,1:T(8,128)S(1)}, f32[512,576]{0,1:T(8,128)S(1)}, u32[]{:S(2)}, u32[]{:S(2)}) collective-permute-start(f32[512,576]{0,1:T(8,128)S(1)} %get-tuple-element.638), channel_id=1, source_target_pairs={{24,0},{32,8},{40,16},{48,24},{56,32},{64,40},{72,48},{80,56},{88,... | collective-permute-start | bytes 3538952 | tf_op jit(solution)/shard_map/ppermute | solution.py:22
  128.0 60.3 %copy-start.3 = (bf16[512,576]{0,1:T(8,128)(2,1)S(1)}, bf16[512,576]{0,1:T(8,128)(2,1)}, u32[]{:S(2)}) copy-start(bf16[512,576]{0,1:T(8,128)(2,1)} %param.11) | copy-start | bytes 1769476
  128.0 58.5 %collective-permute-start.4 = (f32[512,576]{0,1:T(8,128)S(1)}, f32[512,576]{0,1:T(8,128)S(1)}, u32[]{:S(2)}, u32[]{:S(2)}) collective-permute-start(f32[512,576]{0,1:T(8,128)S(1)} %get-tuple-element.639), channel_id=1, source_target_pairs={{16,0},{24,8},{32,16},{40,24},{48,32},{56,40},{64,48},{72,56},{80,... | collective-permute-start | bytes 3538952 | tf_op jit(solution)/shard_map/ppermute | solution.py:22
Sparse Core Ops, SparseCore 0:
  192.5 130.8 reduce-scatter.3
where the time goes:
time: 334 us; the launch traced here: 330 us
  waiting for transfers between devices  130 us (39%)
  blocking collectives  70 us (21%)
  local copies, waits for them, and re-layouts  48.3 us (14%)
  matrix products  37.2 us (11%)
  starting transfers between devices  16 us (5%)
  between operations  14.3 us (4%)
  other arithmetic  13.3 us (4%)
    ppermute x6, waiting for transfers between devices, from_behind(): lax.ppermute(value, axis, [(source, source + steps) for source in range(i...  70.9 us
    psum x1, blocking collectives, local(): lax.psum(jnp.concatenate([latent_part, rope_grad], axis=1), 'head')  70 us
    unnamed x2, waiting for transfers between devices  59.5 us
    gather x8, local copies, waits for them, and re-layouts, block_parts(): key_docs = jnp.take(doc_ids, jnp.clip(key_pos, 0, token_total - 1))  25.1 us
    ppermute x6, starting transfers between devices, from_behind(): lax.ppermute(value, axis, [(source, source + steps) for source in range(i...  15.9 us
    dot_general x8, matrix products, block_parts(): jnp.einsum('thd,kd->htk', query_rope, key_rope, preferred_element_type=jn...  13.2 us
    unnamed x19, local copies, waits for them, and re-layouts  9.15 us
    slice x8, local copies, waits for them, and re-layouts, block_parts(): pairs = key_rows[:, :kv_width].reshape(KEY_BLOCK, head_count, NOPE + VDIM)  8.67 us
  transfers between devices with their start and end apart: 7, of which 5 were waited for; matrix products, arithmetic and copies ran while one was open for 2% of the time, Pallas kernels for 0%

commit v1 on v0

v1 whole, which is shorter than its diff:
```python
import math

import jax
import jax.numpy as jnp
from jax import lax
from jax.experimental import pallas as pl
from jax.experimental.pallas import tpu as pltpu
from jax.sharding import PartitionSpec as P

NOPE, ROPE, VDIM, LATENT = 128, 64, 128, 512
ROWS = 512
HEADS = 2
BIG = 1e30
MESH = pl.DeviceIdType.MESH
SCALE = 1.0 / math.sqrt(NOPE + ROPE)
WIDE = LATENT + ROPE
F32, BF16 = jnp.float32, jnp.bfloat16


def mm(a, b):
    return jnp.dot(a, b, preferred_element_type=F32)


def body(
    latx, q, do, w, dq_ref, out_ref, gwo_ref,
    kbuf, relay_buf, qcat, qcat_t, do_t, w_t, lat_t, kc_t, e_buf, g_buf, m_ref, l_ref, x_ref, mref,
    dq_t, gw, sbuf, crecv, ysum, yrecv, tbuf, orecv, fin, g1recv, g2buf, g2recv, g3buf, g3recv,
    s_p1, s_rel, s_core, s_y, s_o, s_ag, s_g, r_slot, r_rel, r_core, r_y, r_o, r_ag, r_g,
):
    ctx = lax.axis_index("ctx")
    head = lax.axis_index("head")
    z, xl, co = ctx // 4, (ctx // 2) % 2, ctx % 2
    xh, y = head // 4, head % 4
    chip = ctx // 2

    def dev(z_, xl_, co_, xh_, y_):
        return (z_ * 4 + xl_ * 2 + co_, xh_ * 4 + y_)

    def copy(src, dst, ss, rs, to):
        return pltpu.make_async_remote_copy(
            src_ref=src, dst_ref=dst, send_sem=ss, recv_sem=rs, device_id=to, device_id_type=MESH
        )

    barrier = pltpu.get_barrier_semaphore()
    partners = [(ctx, (head + t) % 8) for t in range(1, 8)]
    partners += [dev(z, 1 - xl, co, u // 4, u % 4) for u in range(8)]
    partners += [dev((z + t) % 8, xl, co, xh, y) for t in range(1, 8)]
    partners += [dev(z, xl, 1 - co, u, y) for u in range(2)]
    partners += [dev(z, 1 - xl, 1 - co, u, y) for u in range(2)]
    for dz in (1, 7):
        partners += [dev((z + dz) % 8, 1 - xl, k, u, y) for k in range(2) for u in range(2)]
        partners += [dev((z + dz) % 8, xl, 1 - co, u, y) for u in range(2)]
        partners += [dev((z + dz) % 8, xl, co, 1 - xh, y)]
    for to in partners:
        pl.semaphore_signal(barrier, inc=1, device_id=to, device_id_type=MESH)

    kbuf[3] = latx[...]
    query_mask = ((latx[:, WIDE:].astype(F32) - 1.0) * BIG).astype(BF16)
    for h in range(HEADS):
        base = h * (NOPE + ROPE)
        qc = jnp.concatenate([q[:, base : base + NOPE + ROPE], query_mask], axis=1)
        qcat[h] = qc
        qcat_t[h] = qc.T
        do_t[h] = do[:, h * VDIM : (h + 1) * VDIM].T
    w_t[...] = w[...].T

    pl.semaphore_wait(barrier, len(partners))

    sibling = dev(z, xl, 1 - co, xh, y)
    first = jnp.where(co == 1, 2, 0)
    direct = jnp.where(xl == 0, jnp.where(co == 0, 2, 0), 1)
    third = 3 - first - direct

    def full():
        slot = jnp.where(co == 0, 2, 0)
        return copy(latx, kbuf.at[slot], s_p1.at[0], r_slot.at[slot], dev((z + co) % 8, xl, 1 - co, xh, y))

    def piece():
        rows = pl.ds(pl.multiple_of(head * 64, 64), 64)
        return copy(latx.at[rows], relay_buf, s_p1.at[1], r_rel.at[0], dev((z + 1) % 8, 1, 1 - co, xh, y))

    def half(d):
        rows = pl.ds(d * 256, 256)
        return copy(latx.at[rows], kbuf.at[1, rows], s_p1.at[2 + d], r_slot.at[1], dev(z, 1, co, (xh + d) % 2, y))

    def relay(t):
        slot = jnp.where(co == 0, 2, 0)
        rows = pl.ds(pl.multiple_of(head * 64, 64), 64)
        return copy(relay_buf, kbuf.at[slot, rows], s_rel.at[t], r_slot.at[slot], (z * 4 + co, (head + t) % 8))

    def forward():
        slot = jnp.where(xl == 0, 1, jnp.where(co == 0, 0, 2))
        return copy(kbuf.at[direct], kbuf.at[slot], s_p1.at[4], r_slot.at[slot], sibling)

    @pl.when(xl == 1)
    def _():
        piece().start()

    full().start()

    @pl.when(xl == 0)
    def _():
        half(0).start()
        half(1).start()

    def wait_slot(s):
        copy(latx, kbuf.at[s], s_p1.at[0], r_slot.at[s], sibling).wait_recv()

    def stream(s, own):
        lat = kbuf[s, :, :LATENT]
        tail = kbuf[s, :, LATENT:]
        kv = mm(lat, w[...]).astype(BF16)
        lat_t[s] = lat.T
        for h in range(HEADS):
            base = h * (NOPE + VDIM)
            kc = jnp.concatenate([kv[:, base : base + NOPE], tail], axis=1)
            kc_t[s, h] = kc.T
            scores = mm(kc, qcat_t[h]) * (SCALE * math.log2(math.e))
            if own:
                key = lax.broadcasted_iota(jnp.int32, (ROWS, ROWS), 0)
                query = lax.broadcasted_iota(jnp.int32, (ROWS, ROWS), 1)
                scores = jnp.where(key <= query, scores, -BIG)
            top = jnp.max(scores, axis=0, keepdims=True)
            if not own:
                top = jnp.maximum(top, m_ref[h])
            e = jnp.exp2(scores - top)
            g = mm(kv[:, base + NOPE : base + NOPE + VDIM], do_t[h])
            mass = jnp.sum(e, axis=0, keepdims=True)
            cross = jnp.sum(e * g, axis=0, keepdims=True)
            if not own:
                factor = jnp.exp2(m_ref[h] - top)
                mass = mass + l_ref[h] * factor
                cross = cross + x_ref[h] * factor
            m_ref[h] = top
            l_ref[h] = mass
            x_ref[h] = cross
            mref[s, h] = top
            e_buf[s, h] = e
            g_buf[s, h] = g

    @pl.when(xl == 1)
    def _():
        piece().wait_recv()
        for t in range(8):
            relay(t).start()

    stream(3, True)
    wait_slot(first)
    stream(first, False)
    wait_slot(direct)
    forward().start()
    stream(direct, False)
    wait_slot(third)
    stream(third, False)

    zero = jnp.zeros((256, WIDE), BF16)

    @pl.when(co == 0)
    def _():
        crecv[0] = zero
        sbuf[4, 0] = zero
        orecv[:, 2] = jnp.zeros((2, 2, 32, WIDE), BF16)

    @pl.when(co == 1)
    def _():
        crecv[4] = zero
        sbuf[0, 1] = zero

    def second(s):
        grad_rope = None
        parts = []
        for h in range(HEADS):
            inverse = 1.0 / l_ref[h]
            delta = x_ref[h] * inverse
            p = e_buf[s, h] * (jnp.exp2(mref[s, h] - m_ref[h]) * inverse)
            ds = (p * (g_buf[s, h] - delta)).astype(BF16)
            pb = p.astype(BF16)
            grad_q = mm(kc_t[s, h], ds)
            if s == 0:
                dq_t[h] = grad_q
            else:
                dq_t[h] += grad_q
            grad_k = mm(ds, qcat[h]) * SCALE
            grad_v = mm(pb, do[:, h * VDIM : (h + 1) * VDIM])
            parts += [grad_k[:, :NOPE], grad_v]
            rope = grad_k[:, NOPE : NOPE + ROPE]
            grad_rope = rope if grad_rope is None else grad_rope + rope
        dkv = jnp.concatenate(parts, axis=1).astype(BF16)
        grad = jnp.concatenate([mm(dkv, w_t[...]), grad_rope], axis=1)
        sbuf[s + co] = grad.astype(BF16).reshape(2, 256, WIDE)
        part = mm(lat_t[s], dkv).reshape(16, 2, 16, 512)
        if s == 0:
            gw[...] = part
        else:
            gw[...] += part

    def core_send(s):
        a = s + co
        return copy(sbuf.at[a, 1 - co], crecv.at[a], s_core.at[s], r_core.at[a], sibling)

    def y_send(a, t):
        to = (y + t) % 4
        return copy(ysum.at[a, to], yrecv.at[a, t - 1], s_y.at[a, t - 1], r_y.at[a, t - 1], dev(z, xl, co, xh, to))

    def finish(a):
        def wait():
            copy(sbuf.at[a, 0], crecv.at[a], s_core.at[0], r_core.at[a], sibling).wait_recv()

        if a == 0:
            pl.when(co == 1)(wait)
        elif a == 4:
            pl.when(co == 0)(wait)
        else:
            wait()
        total = sbuf[a, co].astype(F32) + crecv[a].astype(F32)
        ysum[a] = total.astype(BF16).reshape(4, 64, WIDE)
        for t in (2, 1, 3):
            y_send(a, t).start()

    def o_send(a, d):
        owner = (2 * chip + 29 + a) % 32
        to = (xh + d) % 2
        return copy(
            tbuf.at[a, to], orecv.at[xh, a // 2, co], s_o.at[a, d], r_o.at[xh, a // 2, co], (owner, to * 4 + y)
        )

    def o_each(a, d, remote, here):
        if d == 0 and a >= 3:
            pl.when(co != a - 3)(remote)
            if here is not None:
                pl.when(co == a - 3)(here)
        else:
            remote()

    def stage(a):
        for t in (1, 2, 3):
            y_send(a, t).wait_recv()
        total = ysum[a, y].astype(F32)
        for t in range(3):
            total = total + yrecv[a, t].astype(F32)
        tbuf[a] = total.astype(BF16).reshape(2, 32, WIDE)
        for d in range(2):
            def here():
                orecv[xh, a // 2, co] = tbuf[a, xh]

            o_each(a, d, lambda: o_send(a, d).start(), here)

    def g1():
        return copy(gw.at[:, 1 - co], g1recv, s_g.at[0], r_g.at[0], sibling)

    def g2():
        return copy(g2buf.at[:, 1 - xl], g2recv, s_g.at[1], r_g.at[1], dev(z, 1 - xl, co, xh, y))

    def g3(t):
        to = (z + t) % 8
        return copy(g3buf.at[to], g3recv.at[t - 1], s_g.at[1 + t], r_g.at[1 + t], dev(to, xl, co, xh, y))

    for s in range(4):
        second(s)
        core_send(s).start()
        if s:
            finish(s - 1)
    g1().start()
    finish(3)
    g1().wait_recv()
    g2buf[...] = (gw[:, co] + g1recv[...]).astype(BF16).reshape(8, 2, 16, 512)
    g2().start()
    finish(4)
    stage(0)
    for h in range(HEADS):
        dq_ref[:, h * 192 : (h + 1) * 192] = (dq_t[h] * SCALE).T[:, :192].astype(BF16)
    stage(1)
    g2().wait_recv()
    g3buf[...] = (g2buf[:, xl].astype(F32) + g2recv[...].astype(F32)).astype(BF16)
    for t in range(1, 8):
        g3(t).start()
    stage(2)
    stage(3)
    stage(4)
    for t in range(1, 8):
        g3(t).wait_recv()
    total = g3buf[z].astype(F32)
    for t in range(7):
        total = total + g3recv[t].astype(F32)
    gwo_ref[...] = total

    for d in range(2):
        for j in range(3):
            for c in range(2):
                def wait():
                    copy(tbuf.at[0, 0], orecv.at[(xh + d) % 2, j, c], s_o.at[0, 0],
                         r_o.at[(xh + d) % 2, j, c], sibling).wait_recv()

                if d == 0 and j == 1 and c == 0:
                    pl.when(co == 1)(wait)
                elif j == 2 and not (d == 0 and c == 1):
                    pl.when(co == 1)(wait)
                elif j < 2:
                    wait()
    total = orecv[0, 0].astype(F32)
    for k in range(1, 6):
        total = total + orecv[k // 3, k % 3].astype(F32)
    fin[...] = total.astype(BF16)

    def ag(t):
        to = (head + t) % 8
        return copy(fin, out_ref.at[:, y, xh], s_ag.at[t - 1], r_ag.at[t - 1], (ctx, to))

    for t in (2, 6, 1, 7, 3, 5, 4):
        ag(t).start()
    out_ref[:, y, xh] = fin[...]
    for t in range(1, 8):
        ag(t).wait_recv()

    full().wait_send()
    forward().wait_send()

    @pl.when(xl == 1)
    def _():
        piece().wait_send()
        for t in range(8):
            relay(t).wait_send()

    @pl.when(xl == 0)
    def _():
        half(0).wait_send()
        half(1).wait_send()

    for s in range(4):
        core_send(s).wait_send()
    for a in range(5):
        for t in (1, 2, 3):
            y_send(a, t).wait_send()
        for d in range(2):
            o_each(a, d, lambda: o_send(a, d).wait_send(), None)
    g1().wait_send()
    g2().wait_send()
    for t in range(1, 8):
        g3(t).wait_send()
        ag(t).wait_send()


def local(kv_latent, queries, grad_out, kv_up_weight, doc_ids):
    first_row = lax.axis_index("ctx") * ROWS
    docs = lax.dynamic_slice_in_dim(doc_ids, first_row, ROWS)
    marks = (docs[:, None] == jnp.arange(64, dtype=jnp.int32)[None, :]).astype(BF16)
    latx = jnp.concatenate([kv_latent, marks], axis=1)
    vm = pl.BlockSpec(memory_space=pltpu.VMEM)
    dma = pltpu.SemaphoreType.DMA
    V = pltpu.VMEM
    dq, out, gwo = pl.pallas_call(
        body,
        out_shape=(
            jax.ShapeDtypeStruct((ROWS, HEADS * (NOPE + ROPE)), BF16),
            jax.ShapeDtypeStruct((2, 4, 2, 32, WIDE), BF16),
            jax.ShapeDtypeStruct((16, 512), F32),
        ),
        in_specs=[vm] * 4,
        out_specs=(vm, vm, vm),
        scratch_shapes=[
            V((4, ROWS, 640), BF16), V((64, 640), BF16), V((2, ROWS, 256), BF16), V((2, 256, ROWS), BF16),
            V((2, 128, ROWS), BF16), V((512, 512), BF16), V((4, 512, ROWS), BF16), V((4, 2, 256, ROWS), BF16),
            V((4, 2, ROWS, ROWS), F32), V((4, 2, ROWS, ROWS), F32),
            V((2, 1, ROWS), F32), V((2, 1, ROWS), F32), V((2, 1, ROWS), F32), V((4, 2, 1, ROWS), F32),
            V((2, 256, ROWS), F32), V((16, 2, 16, 512), F32),
            V((5, 2, 256, WIDE), BF16), V((5, 256, WIDE), BF16), V((5, 4, 64, WIDE), BF16), V((5, 3, 64, WIDE), BF16),
            V((5, 2, 32, WIDE), BF16), V((2, 3, 2, 32, WIDE), BF16), V((2, 32, WIDE), BF16),
            V((16, 16, 512), F32), V((8, 2, 16, 512), BF16), V((8, 16, 512), BF16), V((8, 16, 512), BF16),
            V((7, 16, 512), BF16),
            dma((5,)), dma((8,)), dma((4,)), dma((5, 3)), dma((5, 2)), dma((7,)), dma((9,)),
            dma((4,)), dma((1,)), dma((5,)), dma((5, 3)), dma((2, 3, 2)), dma((7,)), dma((9,)),
        ],
        compiler_params=pltpu.CompilerParams(
            collective_id=0, has_side_effects=True, vmem_limit_bytes=56 * 1024 * 1024
        ),
        cost_estimate=pl.CostEstimate(flops=7_000_000_000, bytes_accessed=4_000_000, transcendentals=2_100_000),
    )(latx, queries, grad_out, kv_up_weight)
    return dq, out.reshape(ROWS, WIDE), gwo


def solution(mesh):
    return jax.shard_map(
        local,
        mesh=mesh,
        in_specs=(P("ctx", None), P("ctx", "head"), P("ctx", "head"), P(None, "head"), P()),
        out_specs=(P("ctx", "head"), P("ctx", None), P("ctx", "head")),
        check_vma=False,
    )
```

time: 334 us -> 75.7 us (0.23); the launches traced: 330 us -> 75.5 us
  waiting for transfers between devices: 130 us -> 0 us
  blocking collectives: 70 us -> 0 us
  Pallas kernels: 0 us -> 68 us
  local copies, waits for them, and re-layouts: 48.3 us -> 5.68 us
  matrix products: 37.2 us -> 0 us
  starting transfers between devices: 16 us -> 0 us
  between operations: 14.3 us -> 0.67 us
  other arithmetic: 13.3 us -> 1.09 us
    ppermute x6 -> x0, waiting for transfers between devices: 70.9 us -> none  [from_behind(): lax.ppermute(value, axis, [(source, source + steps) for source in range(i...]
    psum x1 -> x0, blocking collectives: 70 us -> none  [local(): lax.psum(jnp.concatenate([latent_part, rope_grad], axis=1), 'head')]
    pallas_call x0 -> x1, Pallas kernels: none -> 68 us  [local(): pl.pallas_call(body, out_shape=(jax.ShapeDtypeStruct((ROWS, HEADS * (NOPE...]
    unnamed x2 -> x0, waiting for transfers between devices: 59.5 us -> none
    dot_general x47 -> x0, matrix products: 37.2 us -> none  [the longest x8 13.2 us: block_parts(): jnp.einsum('thd,kd->htk', query_rope, key_rope, preferred_element_type=jn...]
    gather x8 -> x0, local copies, waits for them, and re-layouts: 25.1 us -> none  [block_parts(): key_docs = jnp.take(doc_ids, jnp.clip(key_pos, 0, token_total - 1))]
    ppermute x6 -> x0, starting transfers between devices: 15.9 us -> none  [from_behind(): lax.ppermute(value, axis, [(source, source + steps) for source in range(i...]
    slice x13 -> x0, local copies, waits for them, and re-layouts: 11.1 us -> none  [the longest x8 8.67 us: block_parts(): pairs = key_rows[:, :kv_width].reshape(KEY_BLOCK, head_count, NOPE + VDIM)]
  transfers between devices with their start and end apart: 7 -> 0, of which waited for: 5 -> 0; matrix products, arithmetic and copies ran while one was open for 2% -> 0% of each run, Pallas kernels for 0% -> 0%
where the time goes in v1:
time: 75.7 us; the launch traced here: 75.5 us
  Pallas kernels  68 us (90%)
  local copies, waits for them, and re-layouts  5.68 us (8%)
  other arithmetic  1.09 us (1%)
    pallas_call x1, Pallas kernels, local(): pl.pallas_call(body, out_shape=(jax.ShapeDtypeStruct((ROWS, HEADS * (NOPE...  68 us
    unnamed x8, local copies, waits for them, and re-layouts  4.91 us

profile of v1, /device:TPU:1, one launch (start us, length us, event | category | flops | bytes accessed | tf_op | source)
XLA Modules:
  0.0 75.5 jit_solution(16288783921356744074)
XLA Ops:
  0.6 0.8 %dynamic_slice.3 = s32[512]{0:T(512)S(1)} dynamic-slice(s32[16384]{0:T(1024)} %param.9, s32[]{:T(128)S(6)} %select_n.3), dynamic_slice_sizes={512} | dynamic-slice | bytes 4100 | tf_op jit(solution)/shard_map/dynamic_slice | solution.py:345
  1.4 0.1 fusion
  1.5 1.4 %copy.8 = bf16[512,576]{1,0:T(8,128)(2,1)S(1)} copy(bf16[512,576]{0,1:T(8,128)(2,1)} %param.5) | data formatting | bytes 1179648 | tf_op args[0]
  2.9 1.0 %pad_maximum_fusion.latx = bf16[512,640]{1,0:T(8,128)(2,1)} fusion(bf16[512,64]{1,0:T(8,128)(2,1)S(1)} %fusion, bf16[512,576]{1,0:T(8,128)(2,1)S(1)} %copy.8), kind=kLoop, calls=%fused_computation | loop fusion | flops 1310720 | bytes 1310720 | tf_op jit(solution)/shard_map/concatenate | solution.py:347
  3.9 68.0 %shard_map.76 = (bf16[512,384]{1,0:T(8,128)(2,1)}, bf16[2,4,2,32,576]{4,3,2,1,0:T(8,128)(2,1)}, f32[16,512]{1,0:T(8,128)}) custom-call(bf16[512,640]{1,0:T(8,128)(2,1)} %pad_maximum_fusion.latx, bf16[512,384]{1,0:T(8,128)(2,1)} %q.1, bf16[512,256]{1,0:T(8,128)(2,1)} %do.1, bf16[512,512]{1,0:T(8,128)(2,1)} %w.1), custom_call_target="tpu_custom_call" | custom-call | flops 7000000000 | bytes 4000000 | tf_op jit(solution)/shard_map/pallas_call | solution.py:351
  71.9 0.0 copy-start
  71.9 2.2 %copy.9 = bf16[512,576]{0,1:T(8,128)(2,1)} copy(bf16[512,576]{1,0:T(8,128)(2,1)} %bitcast.1) | data formatting | bytes 1179648
  74.1 0.0 copy-done
  74.1 0.0 copy-start.1
  74.1 0.7 copy.12
  74.8 0.0 copy-done.1
  74.8 0.6 copy.13
Async XLA Ops:
  71.9 2.2 %copy-start = (bf16[512,384]{1,0:T(8,128)(2,1)S(1)}, bf16[512,384]{1,0:T(8,128)(2,1)}, u32[]{:S(2)}) copy-start(bf16[512,384]{1,0:T(8,128)(2,1)} %get-tuple-element.15) | copy-start | bytes 1179652
  74.1 0.8 %copy-start.1 = (f32[16,512]{1,0:T(8,128)S(1)}, f32[16,512]{1,0:T(8,128)}, u32[]{:S(2)}) copy-start(f32[16,512]{1,0:T(8,128)} %get-tuple-element.17) | copy-start | bytes 98308

commit v2 on v1

v2 whole, which is shorter than its diff:
```python
import math

import jax
import jax.numpy as jnp
from jax import lax
from jax.experimental import pallas as pl
from jax.experimental.pallas import tpu as pltpu
from jax.sharding import PartitionSpec as P

NOPE, ROPE, VDIM, LATENT = 128, 64, 128, 512
ROWS = 512
HEADS = 2
BIG = 1e30
MESH = pl.DeviceIdType.MESH
SCALE = 1.0 / math.sqrt(NOPE + ROPE)
WIDE = LATENT + ROPE
MARKS = 32
KEY_ROWS = WIDE + MARKS
X_FIRST = (1, 3)
F32, BF16 = jnp.float32, jnp.bfloat16


def mm(a, b):
    return jnp.dot(a, b, preferred_element_type=F32)


def body(
    lat_hbm, q_hbm, do_hbm, w_hbm, docs_hbm, dq_ref, out_ref, gwo_ref,
    kbuf, relay_buf, zrecv, q, do, w, docs, qcat, q_t, do_t, w_t, kc, e_buf, g_buf, m_ref, l_ref, x_ref, mref,
    dq_acc, gw, sbuf, crecv, ysum, yrecv, xrecv, xsum, xyrecv, tbuf, orecv, fin, g1recv, g2buf, g2recv, g3buf, g3recv,
    s_in, s_p1, s_rel, s_fwd, s_z, s_core, s_x, s_y, s_o, s_ag, s_g,
    r_slot, r_rel, r_piece, r_half, r_z, r_core, r_x, r_y, r_o, r_ag, r_g,
):
    ctx = lax.axis_index("ctx")
    head = lax.axis_index("head")
    z, xl, co = ctx // 4, (ctx // 2) % 2, ctx % 2
    xh, y = head // 4, head % 4
    chip = ctx // 2

    def dev(z_, xl_, co_, xh_, y_):
        return (z_ * 4 + xl_ * 2 + co_, xh_ * 4 + y_)

    def copy(src, dst, ss, rs, to):
        return pltpu.make_async_remote_copy(
            src_ref=src, dst_ref=dst, send_sem=ss, recv_sem=rs, device_id=to, device_id_type=MESH
        )

    def lanes(k):
        return pl.ds(pl.multiple_of(k * 128, 128), 128)

    inputs = [
        pltpu.make_async_copy(docs_hbm.at[pl.ds(pl.multiple_of(chip * 8, 8), 8)], docs, s_in.at[0]),
        pltpu.make_async_copy(lat_hbm, kbuf.at[3, pl.ds(0, WIDE)], s_in.at[1]),
        pltpu.make_async_copy(w_hbm, w, s_in.at[2]),
        pltpu.make_async_copy(q_hbm, q, s_in.at[3]),
        pltpu.make_async_copy(do_hbm, do, s_in.at[4]),
    ]
    for c in inputs:
        c.start()

    barrier = pltpu.get_barrier_semaphore()
    partners = [(ctx, (head + t) % 8) for t in range(1, 8)]
    partners += [dev(z, 1 - xl, co, u // 4, u % 4) for u in range(8)]
    partners += [dev((z + t) % 8, xl, co, xh, y) for t in range(1, 8)]
    partners += [dev(z, xl, 1 - co, u, y) for u in range(2)]
    partners += [dev(z, 1 - xl, 1 - co, u, y) for u in range(2)]
    for dz in (1, 7):
        partners += [dev((z + dz) % 8, 1 - xl, k, u, y) for k in range(2) for u in range(2)]
        partners += [dev((z + dz) % 8, xl, 1 - co, u, y) for u in range(2)]
        partners += [dev((z + dz) % 8, xl, co, 1 - xh, y)]
    for to in partners:
        pl.semaphore_signal(barrier, inc=1, device_id=to, device_id_type=MESH)

    inputs[0].wait()
    mine = jnp.where(co == 0, docs[0:4, :], docs[4:8, :])
    mine = jnp.concatenate([mine[i : i + 1, :] for i in range(4)], axis=1)
    marks = (lax.broadcasted_iota(jnp.int32, (MARKS, ROWS), 0) == mine).astype(F32)
    kbuf[3, WIDE:, :] = marks.astype(BF16)
    inputs[1].wait()
    pl.semaphore_wait(barrier, len(partners))

    own = kbuf.at[3]
    sibling = dev(z, xl, 1 - co, xh, y)
    first = jnp.where(co == 1, 2, 0)
    direct = jnp.where(xl == 0, jnp.where(co == 0, 2, 0), 1)
    third = 3 - first - direct

    def full():
        slot = jnp.where(co == 0, 2, 0)
        return copy(own, kbuf.at[slot], s_p1.at[0], r_slot.at[slot], dev((z + co) % 8, xl, 1 - co, xh, y))

    def cut(ref, u):
        rows = pl.ds(pl.multiple_of((u // 4) * 304, 16), 304)
        return ref.at[rows, lanes(u % 4)]

    def piece():
        return copy(cut(own, head), relay_buf, s_p1.at[1], r_rel.at[0], dev((z + 1) % 8, 1, 1 - co, xh, y))

    def half(d):
        cols = pl.ds(d * 256, 256)
        return copy(
            own.at[:, cols], kbuf.at[1, :, cols], s_p1.at[2 + d], r_half.at[d], dev(z, 1, co, (xh + d) % 2, y)
        )

    def relay(t):
        slot = jnp.where(co == 0, 2, 0)
        return copy(
            relay_buf, cut(kbuf.at[slot], head), s_rel.at[t], r_piece.at[t], (z * 4 + co, (head + t) % 8)
        )

    def got_piece(t):
        part = cut(kbuf.at[direct], (head + 8 - t) % 8)
        return copy(part, part, s_rel.at[t], r_piece.at[t], sibling)

    def pass_piece(t):
        u = (head + 8 - t) % 8
        return copy(cut(kbuf.at[direct], u), cut(kbuf.at[1], u), s_fwd.at[t], r_slot.at[1], sibling)

    def pass_half(d):
        cols = pl.ds(d * 256, 256)
        slot = jnp.where(co == 0, 0, 2)
        return copy(kbuf.at[1, :, cols], kbuf.at[slot, :, cols], s_fwd.at[d], r_slot.at[slot], sibling)

    late = (xl == 1) & (co == 1)

    @pl.when(xl == 1)
    def _():
        piece().start()

    @pl.when(jnp.logical_not(late))
    def _():
        full().start()

    @pl.when(xl == 0)
    def _():
        half(0).start()
        half(1).start()

    def wait_slot(s):
        copy(own, kbuf.at[s], s_p1.at[0], r_slot.at[s], sibling).wait_recv()

    for c in inputs[2:]:
        c.wait()
    w_t[...] = w[...].T
    query_mask = ((marks.T - 1.0) * BIG).astype(BF16)
    for h in range(HEADS):
        qh = q[:, h * (NOPE + ROPE) : (h + 1) * (NOPE + ROPE)]
        qcat[h] = jnp.concatenate([qh, query_mask], axis=1)
        q_t[h] = qh.T
        do_t[h] = do[:, h * VDIM : (h + 1) * VDIM].T

    @pl.when(late)
    def _():
        piece().wait_send()
        full().start()

    def stream(s, diagonal):
        tail = kbuf[s, LATENT:, :]
        kv = mm(w_t[...], kbuf[s, :LATENT, :]).astype(BF16)
        for h in range(HEADS):
            base = h * (NOPE + VDIM)
            keys = jnp.concatenate([kv[base : base + NOPE], tail], axis=0)
            kc[s, h] = keys[: NOPE + ROPE].T
            scores = mm(qcat[h], keys) * (SCALE * math.log2(math.e))
            if diagonal:
                query = lax.broadcasted_iota(jnp.int32, (ROWS, ROWS), 0)
                key = lax.broadcasted_iota(jnp.int32, (ROWS, ROWS), 1)
                scores = jnp.where(key <= query, scores, -BIG)
            top = jnp.max(scores, axis=1, keepdims=True)
            if not diagonal:
                top = jnp.maximum(top, m_ref[h])
            e = jnp.exp2(scores - top)
            g = mm(do[:, h * VDIM : (h + 1) * VDIM], kv[base + NOPE : base + NOPE + VDIM])
            mass = jnp.sum(e, axis=1, keepdims=True)
            cross = jnp.sum(e * g, axis=1, keepdims=True)
            if not diagonal:
                factor = jnp.exp2(m_ref[h] - top)
                mass = mass + l_ref[h] * factor
                cross = cross + x_ref[h] * factor
            m_ref[h] = top
            l_ref[h] = mass
            x_ref[h] = cross
            mref[s, h] = top
            e_buf[s, h] = e
            g_buf[s, h] = g

    @pl.when(xl == 1)
    def _():
        piece().wait_recv()
        for t in (2, 6, 1, 3, 5, 7, 4, 0):
            relay(t).start()

    stream(3, True)
    wait_slot(first)
    stream(first, False)

    @pl.when(xl == 0)
    def _():
        for t in (0, 4, 1, 3, 5, 7, 2, 6):
            got_piece(t).wait_recv()
            pass_piece(t).start()

    @pl.when(xl == 1)
    def _():
        for d in range(2):
            half(d).wait_recv()
            pass_half(d).start()

    stream(direct, False)
    wait_slot(third)
    stream(third, False)

    @pl.when(co == 0)
    def _():
        sbuf[4, 0] = jnp.zeros((2, 144, 512), BF16)

    @pl.when(co == 1)
    def _():
        crecv[4] = jnp.zeros((2, 144, 512), BF16)

    def second(i):
        s = jnp.where(co == 0, (0, 1, 3, 2)[i], (0, 2, 1, 3)[i])
        grad_rope = None
        parts = []
        for h in range(HEADS):
            inverse = 1.0 / l_ref[h]
            delta = x_ref[h] * inverse
            p = e_buf[s, h] * (jnp.exp2(mref[s, h] - m_ref[h]) * inverse)
            ds = (p * (g_buf[s, h] - delta)).astype(BF16)
            pb = p.astype(BF16)
            grad_q = mm(ds, kc[s, h])
            if i == 0:
                dq_acc[h] = grad_q
            else:
                dq_acc[h] += grad_q
            grad_k = mm(q_t[h], ds) * SCALE
            grad_v = mm(do_t[h], pb)
            parts += [grad_k[:NOPE], grad_v]
            rope = grad_k[NOPE:]
            grad_rope = rope if grad_rope is None else grad_rope + rope
        dkv = jnp.concatenate(parts, axis=0).astype(BF16)
        grad = jnp.concatenate([mm(w[...], dkv), grad_rope], axis=0)
        sbuf[s + co] = grad.astype(BF16).reshape(2, 2, 144, 512)
        part = lax.dot_general(
            kbuf[s, :LATENT, :], dkv, (((1,), (1,)), ((), ())), preferred_element_type=F32
        ).reshape(16, 2, 16, 512)
        if i == 0:
            gw[...] = part
        else:
            gw[...] += part

    def core_send(i):
        a = jnp.where(co == 0, (0, 1, 3, 2)[i], (1, 3, 2, 4)[i])
        return copy(sbuf.at[a, 1 - co], crecv.at[a], s_core.at[i], r_core.at[a], sibling)

    def z_send(c):
        return copy(sbuf.at[0, c], zrecv, s_z.at[c], r_z.at[0], dev((z + 7) % 8, xl, c, xh, y))

    def x_send(a):
        return copy(ysum.at[a, 1 - xh], xrecv.at[a], s_x.at[a], r_x.at[a], dev(z, xl, co, 1 - xh, y))

    def y_send(a, t):
        to = (y + t) % 4
        if a in X_FIRST:
            src, dst = xsum.at[a, :, lanes(to)], xyrecv.at[a, t - 1]
        else:
            src, dst = ysum.at[a, :, :, lanes(to)], yrecv.at[a, t - 1]
        return copy(src, dst, s_y.at[a, t - 1], r_y.at[a, t - 1], dev(z, xl, co, xh, to))

    def finish(a):
        def wait():
            copy(sbuf.at[a, 0], crecv.at[a], s_core.at[0], r_core.at[a], sibling).wait_recv()

        total = sbuf[a, co].astype(F32)
        if a == 4:
            pl.when(co == 0)(wait)
            z_send(0).wait_recv()
            total = total + zrecv[...].astype(F32)
        else:
            wait()
        ysum[a] = (total + crecv[a].astype(F32)).astype(BF16)
        if a in X_FIRST:
            x_send(a).start()
        else:
            for t in (2, 1, 3):
                y_send(a, t).start()

    def middle(a):
        x_send(a).wait_recv()
        xsum[a] = (ysum[a, xh].astype(F32) + xrecv[a].astype(F32)).astype(BF16)
        for t in (2, 1, 3):
            y_send(a, t).start()

    def o_send(a, d):
        owner = (2 * chip + 29 + a) % 32
        to = (xh + d) % 2
        src = tbuf.at[a, 0] if a in X_FIRST else tbuf.at[a, to]
        k = (0, 0, 0, 1, 2)[a] + d
        return copy(src, orecv.at[k, co], s_o.at[a, d], r_o.at[k, co], (owner, to * 4 + y))

    def o_each(a, remote, here):
        if a >= 3:
            pl.when(co != a - 3)(lambda: remote(0))
            if here is not None:
                pl.when(co == a - 3)(here)
        else:
            remote(0)
        if a not in X_FIRST:
            remote(1)

    def stage(a):
        for t in (1, 2, 3):
            y_send(a, t).wait_recv()
        if a in X_FIRST:
            total = xsum[a, :, lanes(y)].astype(F32)
            for t in range(3):
                total = total + xyrecv[a, t].astype(F32)
            tbuf[a, 0] = total.astype(BF16)
        else:
            total = ysum[a, :, :, lanes(y)].astype(F32)
            for t in range(3):
                total = total + yrecv[a, t].astype(F32)
            tbuf[a] = total.astype(BF16)

        def here():
            orecv[(0, 0, 0, 1, 2)[a], co] = tbuf[a, 0] if a in X_FIRST else tbuf[a, xh]

        o_each(a, lambda d: o_send(a, d).start(), here)

    def g1():
        return copy(gw.at[:, 1 - co], g1recv, s_g.at[0], r_g.at[0], sibling)

    def g2():
        return copy(g2buf.at[:, 1 - xl], g2recv, s_g.at[1], r_g.at[1], dev(z, 1 - xl, co, xh, y))

    def g3(t):
        to = (z + t) % 8
        return copy(g3buf.at[to], g3recv.at[t - 1], s_g.at[1 + t], r_g.at[1 + t], dev(to, xl, co, xh, y))

    def arrived(k, c):
        copy(tbuf.at[0, 0], orecv.at[k, c], s_o.at[0, 0], r_o.at[k, c], sibling).wait_recv()

    def ag(t):
        return copy(
            fin, out_ref.at[:, xh, :, lanes(y)], s_ag.at[t - 1], r_ag.at[t - 1], (ctx, (head + t) % 8)
        )

    def final(parts):
        for k, c in parts:
            arrived(k, c)
        total = orecv[0].astype(F32)
        for k in range(1, 2 if len(parts) == 3 else 4):
            total = total + orecv[k].astype(F32)
        fin[...] = total.astype(BF16)
        for t in (2, 6, 1, 7, 3, 5, 4):
            ag(t).start()
        out_ref[:, xh, :, lanes(y)] = fin[...]

    second(0)

    @pl.when(co == 0)
    def _():
        z_send(0).start()
        z_send(1).start()

    @pl.when(co == 1)
    def _():
        core_send(0).start()

    second(1)
    core_send(1).start()
    finish(1)
    second(2)
    core_send(2).start()
    finish(3)
    second(3)
    core_send(3).start()
    g1().start()
    finish(2)
    middle(1)
    g1().wait_recv()
    g2buf[...] = (gw[:, co] + g1recv[...]).astype(BF16).reshape(8, 2, 16, 512)
    g2().start()
    finish(4)
    middle(3)
    g2().wait_recv()
    g3buf[...] = (g2buf[:, xl].astype(F32) + g2recv[...].astype(F32)).astype(BF16)
    for t in range(1, 8):
        g3(t).start()
    stage(2)
    stage(1)
    stage(3)
    stage(4)

    @pl.when(co == 0)
    def _():
        final([(0, 0), (0, 1), (1, 1)])

    @pl.when(co == 1)
    def _():
        final([(0, 0), (0, 1), (1, 0), (1, 1), (2, 0), (3, 0), (3, 1)])

    for h in range(HEADS):
        dq_ref[:, h * 192 : (h + 1) * 192] = (dq_acc[h] * SCALE).astype(BF16)
    for t in range(1, 8):
        g3(t).wait_recv()
    total = g3buf[z].astype(F32)
    for t in range(7):
        total = total + g3recv[t].astype(F32)
    gwo_ref[...] = total
    for t in range(1, 8):
        ag(t).wait_recv()

    full().wait_send()
    pl.when((xl == 1) & (co == 0))(lambda: piece().wait_send())

    @pl.when(xl == 1)
    def _():
        for t in range(8):
            relay(t).wait_send()
        for d in range(2):
            pass_half(d).wait_send()

    @pl.when(xl == 0)
    def _():
        half(0).wait_send()
        half(1).wait_send()
        for t in range(8):
            pass_piece(t).wait_send()

    @pl.when(co == 0)
    def _():
        z_send(0).wait_send()
        z_send(1).wait_send()

    @pl.when(co == 1)
    def _():
        core_send(0).wait_send()

    for i in range(1, 4):
        core_send(i).wait_send()
    for a in range(1, 5):
        if a in X_FIRST:
            x_send(a).wait_send()
        for t in (1, 2, 3):
            y_send(a, t).wait_send()
        o_each(a, lambda d: o_send(a, d).wait_send(), None)
    g1().wait_send()
    g2().wait_send()
    for t in range(1, 8):
        g3(t).wait_send()
        ag(t).wait_send()


def place(dq, out, gwo, dq_ref, out_ref, gwo_ref, dq_v, out_v, gwo_v, sem):
    held = ((dq, dq_v, dq_ref), (out, out_v, out_ref), (gwo, gwo_v, gwo_ref))
    come = [pltpu.make_async_copy(a, b, sem.at[0, i]) for i, (a, b, _) in enumerate(held)]
    go = [pltpu.make_async_copy(b, c, sem.at[1, i]) for i, (_, b, c) in enumerate(held)]
    for c in come:
        c.start()
    for i in range(3):
        come[i].wait()
        go[i].start()
    for c in go:
        c.wait()


def local(kv_latent, queries, grad_out, kv_up_weight, doc_ids):
    vm = pl.BlockSpec(memory_space=pltpu.VMEM)
    hbm = pl.BlockSpec(memory_space=pl.ANY)
    dma = pltpu.SemaphoreType.DMA
    V = pltpu.VMEM
    dq, out, gwo = pl.pallas_call(
        body,
        out_shape=(
            jax.ShapeDtypeStruct((ROWS, HEADS * (NOPE + ROPE)), BF16),
            jax.ShapeDtypeStruct((2, 2, 144, ROWS), BF16),
            jax.ShapeDtypeStruct((16, 512), F32),
        ),
        in_specs=[hbm] * 5,
        out_specs=(vm, vm, vm),
        scratch_shapes=[
            V((4, KEY_ROWS, ROWS), BF16), V((304, 128), BF16), V((2, 144, ROWS), BF16),
            V((ROWS, 384), BF16), V((ROWS, 256), BF16), V((512, 512), BF16), V((8, 128), jnp.int32),
            V((2, ROWS, NOPE + ROPE + MARKS), BF16), V((2, 192, ROWS), BF16), V((2, 128, ROWS), BF16), V((512, 512), BF16),
            V((4, 2, ROWS, 192), BF16), V((4, 2, ROWS, ROWS), F32), V((4, 2, ROWS, ROWS), F32),
            V((2, ROWS, 1), F32), V((2, ROWS, 1), F32), V((2, ROWS, 1), F32), V((4, 2, ROWS, 1), F32),
            V((2, ROWS, 192), F32), V((16, 2, 16, 512), F32),
            V((5, 2, 2, 144, 512), BF16), V((5, 2, 144, 512), BF16), V((5, 2, 144, 512), BF16),
            V((5, 3, 2, 144, 128), BF16), V((5, 144, 512), BF16), V((5, 144, 512), BF16), V((5, 3, 144, 128), BF16),
            V((5, 2, 144, 128), BF16), V((4, 2, 144, 128), BF16), V((2, 144, 128), BF16),
            V((16, 16, 512), F32), V((8, 2, 16, 512), BF16), V((8, 16, 512), BF16), V((8, 16, 512), BF16),
            V((7, 16, 512), BF16),
            dma((5,)), dma((4,)), dma((8,)), dma((8,)), dma((2,)), dma((4,)), dma((5,)), dma((5, 3)), dma((5, 2)), dma((7,)),
            dma((9,)),
            dma((3,)), dma((1,)), dma((8,)), dma((2,)), dma((1,)), dma((5,)), dma((5,)), dma((5, 3)), dma((5, 2)), dma((7,)),
            dma((9,)),
        ],
        compiler_params=pltpu.CompilerParams(
            collective_id=0, has_side_effects=True, vmem_limit_bytes=58 * 1024 * 1024
        ),
        cost_estimate=pl.CostEstimate(flops=7_000_000_000, bytes_accessed=4_000_000, transcendentals=2_100_000),
    )(kv_latent.T, queries, grad_out, kv_up_weight, doc_ids.reshape(128, 128))
    dq, out, gwo = pl.pallas_call(
        place,
        out_shape=(
            jax.ShapeDtypeStruct((ROWS, HEADS * (NOPE + ROPE)), BF16),
            jax.ShapeDtypeStruct((WIDE, ROWS), BF16),
            jax.ShapeDtypeStruct((16, 512), F32),
        ),
        in_specs=[hbm] * 3,
        out_specs=(hbm, hbm, hbm),
        scratch_shapes=[V((ROWS, 384), BF16), V((WIDE, ROWS), BF16), V((16, 512), F32), dma((2, 3))],
    )(dq, out.reshape(WIDE, ROWS), gwo)
    return dq, out.T, gwo


def solution(mesh):
    return jax.shard_map(
        local,
        mesh=mesh,
        in_specs=(P("ctx", None), P("ctx", "head"), P("ctx", "head"), P(None, "head"), P()),
        out_specs=(P("ctx", "head"), P("ctx", None), P("ctx", "head")),
        check_vma=False,
    )
```

time: 75.7 us -> 67 us (0.89)
  local copies, waits for them, and re-layouts: 5.68 us -> 0 us
  Pallas kernels: 68 us -> 66.1 us
  other arithmetic: 1.09 us -> 0 us
    unnamed x8 -> x0, local copies, waits for them, and re-layouts: 4.91 us -> none
    pallas_call x1, Pallas kernels: 68 us -> 64 us  [local(): pl.pallas_call(body, out_shape=(jax.ShapeDtypeStruct((ROWS, HEADS * (NOPE...]
    pallas_call x0 -> x1, Pallas kernels: none -> 2.05 us  [local(): pl.pallas_call(place, out_shape=(jax.ShapeDtypeStruct((ROWS, HEADS * (NOP...]
    concatenate x1 -> x0, other arithmetic: 0.95 us -> none  [local(): latx = jnp.concatenate([kv_latent, marks], axis=1)]
    dynamic_slice x1 -> x0, local copies, waits for them, and re-layouts: 0.76 us -> none  [local(): docs = lax.dynamic_slice_in_dim(doc_ids, first_row, ROWS)]
where the time goes in v2:
time: 67 us; the launch traced here: 66.9 us
  Pallas kernels  66.1 us (99%)
  between operations  0.8 us (1%)
    pallas_call x1, Pallas kernels, local(): pl.pallas_call(body, out_shape=(jax.ShapeDtypeStruct((ROWS, HEADS * (NOPE...  64 us
    pallas_call x1, Pallas kernels, local(): pl.pallas_call(place, out_shape=(jax.ShapeDtypeStruct((ROWS, HEADS * (NOP...  2.05 us

profile of v2, /device:TPU:1, one launch (start us, length us, event | category | flops | bytes accessed | tf_op | source)
XLA Modules:
  0.0 66.9 jit_solution(15123905059998809446)
XLA Ops:
  0.6 64.0 %shard_map.76 = (bf16[512,384]{1,0:T(8,128)(2,1)}, bf16[2,2,144,512]{3,2,1,0:T(8,128)(2,1)}, f32[16,512]{1,0:T(8,128)}) custom-call(bf16[576,512]{1,0:T(8,128)(2,1)} %bitcast.5, bf16[512,384]{1,0:T(8,128)(2,1)} %q_hbm.1, bf16[512,256]{1,0:T(8,128)(2,1)} %do_hbm.1, bf16[512,512]{1,0:T(8,128)(2,1)} %w_hbm.1, s32[128,128]{1,0:T(8,128)} %bitcast.7), custom_call_target="tpu_custom_call" | custom-call | flops 7000000000 | bytes 4000000 | tf_op jit(solution)/shard_map/pallas_call | solution.py:473
  64.6 2.1 %shard_map.77 = (bf16[512,384]{1,0:T(8,128)(2,1)}, bf16[576,512]{1,0:T(8,128)(2,1)}, f32[16,512]{1,0:T(8,128)}) custom-call(bf16[512,384]{1,0:T(8,128)(2,1)} %get-tuple-element.9.dq, bf16[576,512]{1,0:T(8,128)(2,1)} %bitcast.4, f32[16,512]{1,0:T(8,128)} %get-tuple-element.11.gwo), custom_call_target="tpu_custom_call" | custom-call | tf_op jit(solution)/shard_map/pallas_call | solution.py:504

commit v3 on v2

--- a/solution.py
+++ b/solution.py
@@ -16,7 +16,8 @@
 WIDE = LATENT + ROPE
 MARKS = 32
 KEY_ROWS = WIDE + MARKS
-X_FIRST = (1, 3)
+X_FIRST = (2,)
+FIRST_PART = (0, 0, 0, 2, 1)
 F32, BF16 = jnp.float32, jnp.bfloat16
 
 
@@ -29,7 +30,7 @@
     kbuf, relay_buf, zrecv, q, do, w, docs, qcat, q_t, do_t, w_t, kc, e_buf, g_buf, m_ref, l_ref, x_ref, mref,
     dq_acc, gw, sbuf, crecv, ysum, yrecv, xrecv, xsum, xyrecv, tbuf, orecv, fin, g1recv, g2buf, g2recv, g3buf, g3recv,
     s_in, s_p1, s_rel, s_fwd, s_z, s_core, s_x, s_y, s_o, s_ag, s_g,
-    r_slot, r_rel, r_piece, r_half, r_z, r_core, r_x, r_y, r_o, r_ag, r_g,
+    r_slot, r_rel, told, r_piece, r_half, r_z, r_core, r_x, r_y, r_o, r_ag, r_g,
 ):
     ctx = lax.axis_index("ctx")
     head = lax.axis_index("head")
@@ -47,6 +48,40 @@
 
     def lanes(k):
         return pl.ds(pl.multiple_of(k * 128, 128), 128)
+
+    barrier = pltpu.get_barrier_semaphore()
+    partners = [(ctx, (head + t) % 8) for t in range(1, 8)]
+    partners += [dev(z, 1 - xl, co, u // 4, u % 4) for u in range(8)]
+    partners += [dev(z, xl, 1 - co, u, y) for u in range(2)]
+    partners += [dev(z, 1 - xl, 1 - co, u, y) for u in range(2)]
+    below, above = z > 0, z < 7
+    beside = jnp.where(xl == 0, below, above)
+
+    def greet(to):
+        pl.semaphore_signal(barrier, inc=1, device_id=to, device_id_type=MESH)
+
+    for to in partners:
+        greet(to)
+
+    @pl.when(below)
+    def _():
+        for k in range(2):
+            greet(dev(z - 1, xl, k, xh, y))
+
+    @pl.when(above)
+    def _():
+        for k in range(2):
+            greet(dev(z + 1, xl, k, xh, y))
+
+    @pl.when(beside)
+    def _():
+        for k in range(2):
+            for u in range(2):
+                greet(dev(z - 1 + 2 * xl, 1 - xl, k, u, y))
+
+    greetings = (
+        len(partners) + jnp.where(below, 2, 0) + jnp.where(above, 2, 0) + jnp.where(beside, 4, 0)
+    )
 
     inputs = [
         pltpu.make_async_copy(docs_hbm.at[pl.ds(pl.multiple_of(chip * 8, 8), 8)], docs, s_in.at[0]),
@@ -58,26 +93,41 @@
     for c in inputs:
         c.start()
 
-    barrier = pltpu.get_barrier_semaphore()
-    partners = [(ctx, (head + t) % 8) for t in range(1, 8)]
-    partners += [dev(z, 1 - xl, co, u // 4, u % 4) for u in range(8)]
-    partners += [dev((z + t) % 8, xl, co, xh, y) for t in range(1, 8)]
-    partners += [dev(z, xl, 1 - co, u, y) for u in range(2)]
-    partners += [dev(z, 1 - xl, 1 - co, u, y) for u in range(2)]
-    for dz in (1, 7):
-        partners += [dev((z + dz) % 8, 1 - xl, k, u, y) for k in range(2) for u in range(2)]
-        partners += [dev((z + dz) % 8, xl, 1 - co, u, y) for u in range(2)]
-        partners += [dev((z + dz) % 8, xl, co, 1 - xh, y)]
-    for to in partners:
-        pl.semaphore_signal(barrier, inc=1, device_id=to, device_id_type=MESH)
-
     inputs[0].wait()
     mine = jnp.where(co == 0, docs[0:4, :], docs[4:8, :])
     mine = jnp.concatenate([mine[i : i + 1, :] for i in range(4)], axis=1)
     marks = (lax.broadcasted_iota(jnp.int32, (MARKS, ROWS), 0) == mine).astype(F32)
     kbuf[3, WIDE:, :] = marks.astype(BF16)
     inputs[1].wait()
-    pl.semaphore_wait(barrier, len(partners))
+    pl.semaphore_wait(barrier, greetings)
+
+    def tell(k):
+        @pl.when(z >= 2**k)
+        def _():
+            pl.semaphore_signal(told.at[k], inc=1, device_id=dev(z - 2**k, xl, co, xh, y), device_id_type=MESH)
+
+        @pl.when(z + 2**k < 8)
+        def _():
+            pl.semaphore_signal(told.at[k], inc=1, device_id=dev(z + 2**k, xl, co, xh, y), device_id_type=MESH)
+
+    def hear(k):
+        pl.semaphore_wait(told.at[k], jnp.where(z >= 2**k, 1, 0) + jnp.where(z + 2**k < 8, 1, 0))
+
+    tell(0)
+
+    for s in range(3):
+        @pl.when((z == 0) & (s < 3 - 2 * xl - co))
+        def _():
+            kbuf[s, :WIDE, :] = jnp.zeros((WIDE, ROWS), BF16)
+            kbuf[s, WIDE:, :] = jnp.ones((MARKS, ROWS), BF16)
+
+    @pl.when(z == 7)
+    def _():
+        zrecv[...] = jnp.zeros((2, 144, ROWS), BF16)
+
+    @pl.when(chip == 15)
+    def _():
+        orecv[0:2] = jnp.zeros((2, 2, 144, 128), BF16)
 
     own = kbuf.at[3]
     sibling = dev(z, xl, 1 - co, xh, y)
@@ -122,12 +172,13 @@
         return copy(kbuf.at[1, :, cols], kbuf.at[slot, :, cols], s_fwd.at[d], r_slot.at[slot], sibling)
 
     late = (xl == 1) & (co == 1)
-
-    @pl.when(xl == 1)
+    sends_full = (co == 0) | above
+
+    @pl.when((xl == 1) & above)
     def _():
         piece().start()
 
-    @pl.when(jnp.logical_not(late))
+    @pl.when(jnp.logical_not(late) & sends_full)
     def _():
         full().start()
 
@@ -149,7 +200,7 @@
         q_t[h] = qh.T
         do_t[h] = do[:, h * VDIM : (h + 1) * VDIM].T
 
-    @pl.when(late)
+    @pl.when(late & above)
     def _():
         piece().wait_send()
         full().start()
@@ -184,17 +235,19 @@
             e_buf[s, h] = e
             g_buf[s, h] = g
 
-    @pl.when(xl == 1)
+    @pl.when((xl == 1) & below)
     def _():
         piece().wait_recv()
         for t in (2, 6, 1, 3, 5, 7, 4, 0):
             relay(t).start()
 
     stream(3, True)
-    wait_slot(first)
+    hear(0)
+    tell(1)
+    pl.when((co == 1) | below)(lambda: wait_slot(first))
     stream(first, False)
 
-    @pl.when(xl == 0)
+    @pl.when((xl == 0) & below)
     def _():
         for t in (0, 4, 1, 3, 5, 7, 2, 6):
             got_piece(t).wait_recv()
@@ -207,7 +260,7 @@
             pass_half(d).start()
 
     stream(direct, False)
-    wait_slot(third)
+    pl.when((xl == 1) | below)(lambda: wait_slot(third))
     stream(third, False)
 
     @pl.when(co == 0)
@@ -218,8 +271,8 @@
     def _():
         crecv[4] = jnp.zeros((2, 144, 512), BF16)
 
-    def second(i):
-        s = jnp.where(co == 0, (0, 1, 3, 2)[i], (0, 2, 1, 3)[i])
+    def second(i, meanwhile=None):
+        s = jnp.where(co == 0, (0, 1, 3, 2)[i], (3, 0, 2, 1)[i])
         grad_rope = None
         parts = []
         for h in range(HEADS):
@@ -239,6 +292,8 @@
             rope = grad_k[NOPE:]
             grad_rope = rope if grad_rope is None else grad_rope + rope
         dkv = jnp.concatenate(parts, axis=0).astype(BF16)
+        if meanwhile is not None:
+            meanwhile()
         grad = jnp.concatenate([mm(w[...], dkv), grad_rope], axis=0)
         sbuf[s + co] = grad.astype(BF16).reshape(2, 2, 144, 512)
         part = lax.dot_general(
@@ -250,7 +305,7 @@
             gw[...] += part
 
     def core_send(i):
-        a = jnp.where(co == 0, (0, 1, 3, 2)[i], (1, 3, 2, 4)[i])
+        a = jnp.where(co == 0, (0, 1, 3, 2)[i], (4, 1, 3, 2)[i])
         return copy(sbuf.at[a, 1 - co], crecv.at[a], s_core.at[i], r_core.at[a], sibling)
 
     def z_send(c):
@@ -274,7 +329,7 @@
         total = sbuf[a, co].astype(F32)
         if a == 4:
             pl.when(co == 0)(wait)
-            z_send(0).wait_recv()
+            pl.when(above)(lambda: z_send(0).wait_recv())
             total = total + zrecv[...].astype(F32)
         else:
             wait()
@@ -295,17 +350,21 @@
         owner = (2 * chip + 29 + a) % 32
         to = (xh + d) % 2
         src = tbuf.at[a, 0] if a in X_FIRST else tbuf.at[a, to]
-        k = (0, 0, 0, 1, 2)[a] + d
+        k = FIRST_PART[a] + d
         return copy(src, orecv.at[k, co], s_o.at[a, d], r_o.at[k, co], (owner, to * 4 + y))
 
     def o_each(a, remote, here):
-        if a >= 3:
+        def both():
+            remote(0)
+            if a not in X_FIRST:
+                remote(1)
+
+        if a < 3:
+            pl.when(chip > 0)(both)
+        else:
             pl.when(co != a - 3)(lambda: remote(0))
             if here is not None:
                 pl.when(co == a - 3)(here)
-        else:
-            remote(0)
-        if a not in X_FIRST:
             remote(1)
 
     def stage(a):
@@ -323,7 +382,7 @@
             tbuf[a] = total.astype(BF16)
 
         def here():
-            orecv[(0, 0, 0, 1, 2)[a], co] = tbuf[a, 0] if a in X_FIRST else tbuf[a, xh]
+            orecv[FIRST_PART[a], co] = tbuf[a, 0] if a in X_FIRST else tbuf[a, xh]
 
         o_each(a, lambda d: o_send(a, d).start(), here)
 
@@ -345,11 +404,16 @@
             fin, out_ref.at[:, xh, :, lanes(y)], s_ag.at[t - 1], r_ag.at[t - 1], (ctx, (head + t) % 8)
         )
 
-    def final(parts):
-        for k, c in parts:
+    def final(count, parts):
+        @pl.when(chip < 15)
+        def _():
+            for k, c in parts[0]:
+                arrived(k, c)
+
+        for k, c in parts[1]:
             arrived(k, c)
         total = orecv[0].astype(F32)
-        for k in range(1, 2 if len(parts) == 3 else 4):
+        for k in range(1, count):
             total = total + orecv[k].astype(F32)
         fin[...] = total.astype(BF16)
         for t in (2, 6, 1, 7, 3, 5, 4):
@@ -358,7 +422,10 @@
 
     second(0)
 
-    @pl.when(co == 0)
+    hear(1)
+    tell(2)
+
+    @pl.when((co == 0) & below)
     def _():
         z_send(0).start()
         z_send(1).start()
@@ -369,36 +436,35 @@
 
     second(1)
     core_send(1).start()
-    finish(1)
-    second(2)
+    second(2, lambda: finish(1))
     core_send(2).start()
-    finish(3)
-    second(3)
+    second(3, lambda: finish(3))
     core_send(3).start()
     g1().start()
     finish(2)
-    middle(1)
     g1().wait_recv()
     g2buf[...] = (gw[:, co] + g1recv[...]).astype(BF16).reshape(8, 2, 16, 512)
     g2().start()
+    stage(1)
     finish(4)
-    middle(3)
+    stage(3)
     g2().wait_recv()
     g3buf[...] = (g2buf[:, xl].astype(F32) + g2recv[...].astype(F32)).astype(BF16)
+    hear(2)
     for t in range(1, 8):
         g3(t).start()
+    middle(2)
+
+    stage(4)
     stage(2)
-    stage(1)
-    stage(3)
-    stage(4)
 
     @pl.when(co == 0)
     def _():
-        final([(0, 0), (0, 1), (1, 1)])
+        final(4, ([(0, 0), (0, 1), (1, 0), (1, 1)], [(2, 1), (3, 0), (3, 1)]))
 
     @pl.when(co == 1)
     def _():
-        final([(0, 0), (0, 1), (1, 0), (1, 1), (2, 0), (3, 0), (3, 1)])
+        final(3, ([(0, 0), (0, 1)], [(1, 0), (2, 0), (2, 1)]))
 
     for h in range(HEADS):
         dq_ref[:, h * 192 : (h + 1) * 192] = (dq_acc[h] * SCALE).astype(BF16)
@@ -411,13 +477,16 @@
     for t in range(1, 8):
         ag(t).wait_recv()
 
-    full().wait_send()
-    pl.when((xl == 1) & (co == 0))(lambda: piece().wait_send())
-
-    @pl.when(xl == 1)
+    pl.when(sends_full)(lambda: full().wait_send())
+    pl.when((xl == 1) & (co == 0) & above)(lambda: piece().wait_send())
+
+    @pl.when((xl == 1) & below)
     def _():
         for t in range(8):
             relay(t).wait_send()
+
+    @pl.when(xl == 1)
+    def _():
         for d in range(2):
             pass_half(d).wait_send()
 
@@ -425,10 +494,13 @@
     def _():
         half(0).wait_send()
         half(1).wait_send()
+
+    @pl.when((xl == 0) & below)
+    def _():
         for t in range(8):
             pass_piece(t).wait_send()
 
-    @pl.when(co == 0)
+    @pl.when((co == 0) & below)
     def _():
         z_send(0).wait_send()
         z_send(1).wait_send()
@@ -493,7 +565,7 @@
             V((7, 16, 512), BF16),
             dma((5,)), dma((4,)), dma((8,)), dma((8,)), dma((2,)), dma((4,)), dma((5,)), dma((5, 3)), dma((5, 2)), dma((7,)),
             dma((9,)),
-            dma((3,)), dma((1,)), dma((8,)), dma((2,)), dma((1,)), dma((5,)), dma((5,)), dma((5, 3)), dma((5, 2)), dma((7,)),
+            dma((3,)), dma((1,)), pltpu.SemaphoreType.REGULAR((3,)), dma((8,)), dma((2,)), dma((1,)), dma((5,)), dma((5,)), dma((5, 3)), dma((5, 2)), dma((7,)),
             dma((9,)),
         ],
         compiler_params=pltpu.CompilerParams(

time: 67 us -> 61.5 us (0.918)
  the two profiles are of different devices: /device:TPU:1 before, /device:TPU:129 now
where the time goes in v3:
time: 61.5 us; the launch traced here: 61.4 us
  Pallas kernels  60.6 us (99%)
  between operations  0.8 us (1%)
    pallas_call x1, Pallas kernels, local(): pl.pallas_call(body, out_shape=(jax.ShapeDtypeStruct((ROWS, HEADS * (NOPE...  58.5 us
    pallas_call x1, Pallas kernels, local(): pl.pallas_call(place, out_shape=(jax.ShapeDtypeStruct((ROWS, HEADS * (NOP...  2.05 us

profile of v3, /device:TPU:129, one launch (start us, length us, event | category | flops | bytes accessed | tf_op | source)
XLA Modules:
  0.0 61.4 jit_solution(1877685099406157109)
XLA Ops:
  0.6 58.5 %shard_map.76 = (bf16[512,384]{1,0:T(8,128)(2,1)}, bf16[2,2,144,512]{3,2,1,0:T(8,128)(2,1)}, f32[16,512]{1,0:T(8,128)}) custom-call(bf16[576,512]{1,0:T(8,128)(2,1)} %bitcast.5, bf16[512,384]{1,0:T(8,128)(2,1)} %q_hbm.1, bf16[512,256]{1,0:T(8,128)(2,1)} %do_hbm.1, bf16[512,512]{1,0:T(8,128)(2,1)} %w_hbm.1, s32[128,128]{1,0:T(8,128)} %bitcast.7), custom_call_target="tpu_custom_call" | custom-call | flops 7000000000 | bytes 4000000 | tf_op jit(solution)/shard_map/pallas_call | solution.py:545
  59.2 2.1 %shard_map.77 = (bf16[512,384]{1,0:T(8,128)(2,1)}, bf16[576,512]{1,0:T(8,128)(2,1)}, f32[16,512]{1,0:T(8,128)}) custom-call(bf16[512,384]{1,0:T(8,128)(2,1)} %get-tuple-element.9.dq, bf16[576,512]{1,0:T(8,128)(2,1)} %bitcast.4, f32[16,512]{1,0:T(8,128)} %get-tuple-element.11.gwo), custom_call_target="tpu_custom_call" | custom-call | tf_op jit(solution)/shard_map/pallas_call | solution.py:576

commit v4 on v3

--- a/solution.py
+++ b/solution.py
@@ -16,8 +16,7 @@
 WIDE = LATENT + ROPE
 MARKS = 32
 KEY_ROWS = WIDE + MARKS
-X_FIRST = (2,)
-FIRST_PART = (0, 0, 0, 2, 1)
+FIRST_PART = (0, 0, 0, 2, 2)
 F32, BF16 = jnp.float32, jnp.bfloat16
 
 
@@ -26,11 +25,11 @@
 
 
 def body(
-    lat_hbm, q_hbm, do_hbm, w_hbm, docs_hbm, dq_ref, out_ref, gwo_ref,
-    kbuf, relay_buf, zrecv, q, do, w, docs, qcat, q_t, do_t, w_t, kc, e_buf, g_buf, m_ref, l_ref, x_ref, mref,
-    dq_acc, gw, sbuf, crecv, ysum, yrecv, xrecv, xsum, xyrecv, tbuf, orecv, fin, g1recv, g2buf, g2recv, g3buf, g3recv,
-    s_in, s_p1, s_rel, s_fwd, s_z, s_core, s_x, s_y, s_o, s_ag, s_g,
-    r_slot, r_rel, told, r_piece, r_half, r_z, r_core, r_x, r_y, r_o, r_ag, r_g,
+    lat_hbm, q_hbm, do_hbm, w_hbm, docs_hbm, dq_hbm, out_ref, gwo_hbm,
+    dq_ref, gwo_ref, s_out, kbuf, relay_buf, zrecv, q, do, w, docs, qcat, q_t, do_t, w_t, kc, e_buf, g_buf, m_ref, l_ref, x_ref, mref,
+    dq_acc, gw, sbuf, crecv, ysum, yrecv, tbuf, orecv, fin, g1recv, g2buf, g2recv, g3buf, g3recv,
+    s_in, s_p1, s_rel, s_fwd, s_z, s_core, s_y, s_o, s_ag, s_g,
+    r_slot, r_rel, told, r_piece, r_half, r_z, r_core, r_y, r_o, r_ag, r_g,
 ):
     ctx = lax.axis_index("ctx")
     head = lax.axis_index("head")
@@ -48,6 +47,16 @@
 
     def lanes(k):
         return pl.ds(pl.multiple_of(k * 128, 128), 128)
+
+    inputs = [
+        pltpu.make_async_copy(docs_hbm.at[pl.ds(pl.multiple_of(chip * 8, 8), 8)], docs, s_in.at[0]),
+        pltpu.make_async_copy(lat_hbm, kbuf.at[3, pl.ds(0, WIDE)], s_in.at[1]),
+        pltpu.make_async_copy(w_hbm, w, s_in.at[2]),
+        pltpu.make_async_copy(q_hbm, q, s_in.at[3]),
+        pltpu.make_async_copy(do_hbm, do, s_in.at[4]),
+    ]
+    for c in inputs[:2]:
+        c.start()
 
     barrier = pltpu.get_barrier_semaphore()
     partners = [(ctx, (head + t) % 8) for t in range(1, 8)]
@@ -83,14 +92,7 @@
         len(partners) + jnp.where(below, 2, 0) + jnp.where(above, 2, 0) + jnp.where(beside, 4, 0)
     )
 
-    inputs = [
-        pltpu.make_async_copy(docs_hbm.at[pl.ds(pl.multiple_of(chip * 8, 8), 8)], docs, s_in.at[0]),
-        pltpu.make_async_copy(lat_hbm, kbuf.at[3, pl.ds(0, WIDE)], s_in.at[1]),
-        pltpu.make_async_copy(w_hbm, w, s_in.at[2]),
-        pltpu.make_async_copy(q_hbm, q, s_in.at[3]),
-        pltpu.make_async_copy(do_hbm, do, s_in.at[4]),
-    ]
-    for c in inputs:
+    for c in inputs[2:]:
         c.start()
 
     inputs[0].wait()
@@ -113,6 +115,67 @@
     def hear(k):
         pl.semaphore_wait(told.at[k], jnp.where(z >= 2**k, 1, 0) + jnp.where(z + 2**k < 8, 1, 0))
 
+    own = kbuf.at[3]
+    sibling = dev(z, xl, 1 - co, xh, y)
+    first = jnp.where(co == 1, 2, 0)
+    direct = jnp.where(xl == 0, jnp.where(co == 0, 2, 0), 1)
+    third = 3 - first - direct
+
+    def full():
+        slot = jnp.where(co == 0, 2, 0)
+        return copy(own, kbuf.at[slot], s_p1.at[0], r_slot.at[slot], dev((z + co) % 8, xl, 1 - co, xh, y))
+
+    def cut(ref, u):
+        rows = pl.ds(pl.multiple_of((u // 4) * 304, 16), 304)
+        return ref.at[rows, lanes(u % 4)]
+
+    def piece():
+        return copy(cut(own, head), relay_buf, s_p1.at[1], r_rel.at[0], dev((z + 1) % 8, 1, 1 - co, xh, y))
+
+    def half(d):
+        cols = pl.ds(d * 256, 256)
+        return copy(
+            own.at[:, cols], kbuf.at[1, :, cols], s_p1.at[2 + d], r_half.at[d], dev(z, 1, co, (xh + d) % 2, y)
+        )
+
+    def relay(t):
+        slot = jnp.where(co == 0, 2, 0)
+        return copy(
+            relay_buf, cut(kbuf.at[slot], head), s_rel.at[t], r_piece.at[t], (z * 4 + co, (head + t) % 8)
+        )
+
+    def got_piece(t):
+        part = cut(kbuf.at[direct], (head + 8 - t) % 8)
+        return copy(part, part, s_rel.at[t], r_piece.at[t], sibling)
+
+    def pass_piece(t):
+        u = (head + 8 - t) % 8
+        return copy(cut(kbuf.at[direct], u), cut(kbuf.at[1], u), s_fwd.at[t], r_slot.at[1], sibling)
+
+    def pass_half(d):
+        cols = pl.ds(d * 256, 256)
+        slot = jnp.where(co == 0, 0, 2)
+        return copy(kbuf.at[1, :, cols], kbuf.at[slot, :, cols], s_fwd.at[d], r_slot.at[slot], sibling)
+
+    late = (xl == 1) & (co == 1)
+    sends_full = (co == 0) | above
+
+    @pl.when((xl == 1) & above)
+    def _():
+        piece().start()
+
+    @pl.when(jnp.logical_not(late) & sends_full)
+    def _():
+        full().start()
+
+    @pl.when(xl == 0)
+    def _():
+        half(0).start()
+        half(1).start()
+
+    def wait_slot(s):
+        copy(own, kbuf.at[s], s_p1.at[0], r_slot.at[s], sibling).wait_recv()
+
     tell(0)
 
     for s in range(3):
@@ -128,67 +191,6 @@
     @pl.when(chip == 15)
     def _():
         orecv[0:2] = jnp.zeros((2, 2, 144, 128), BF16)
-
-    own = kbuf.at[3]
-    sibling = dev(z, xl, 1 - co, xh, y)
-    first = jnp.where(co == 1, 2, 0)
-    direct = jnp.where(xl == 0, jnp.where(co == 0, 2, 0), 1)
-    third = 3 - first - direct
-
-    def full():
-        slot = jnp.where(co == 0, 2, 0)
-        return copy(own, kbuf.at[slot], s_p1.at[0], r_slot.at[slot], dev((z + co) % 8, xl, 1 - co, xh, y))
-
-    def cut(ref, u):
-        rows = pl.ds(pl.multiple_of((u // 4) * 304, 16), 304)
-        return ref.at[rows, lanes(u % 4)]
-
-    def piece():
-        return copy(cut(own, head), relay_buf, s_p1.at[1], r_rel.at[0], dev((z + 1) % 8, 1, 1 - co, xh, y))
-
-    def half(d):
-        cols = pl.ds(d * 256, 256)
-        return copy(
-            own.at[:, cols], kbuf.at[1, :, cols], s_p1.at[2 + d], r_half.at[d], dev(z, 1, co, (xh + d) % 2, y)
-        )
-
-    def relay(t):
-        slot = jnp.where(co == 0, 2, 0)
-        return copy(
-            relay_buf, cut(kbuf.at[slot], head), s_rel.at[t], r_piece.at[t], (z * 4 + co, (head + t) % 8)
-        )
-
-    def got_piece(t):
-        part = cut(kbuf.at[direct], (head + 8 - t) % 8)
-        return copy(part, part, s_rel.at[t], r_piece.at[t], sibling)
-
-    def pass_piece(t):
-        u = (head + 8 - t) % 8
-        return copy(cut(kbuf.at[direct], u), cut(kbuf.at[1], u), s_fwd.at[t], r_slot.at[1], sibling)
-
-    def pass_half(d):
-        cols = pl.ds(d * 256, 256)
-        slot = jnp.where(co == 0, 0, 2)
-        return copy(kbuf.at[1, :, cols], kbuf.at[slot, :, cols], s_fwd.at[d], r_slot.at[slot], sibling)
-
-    late = (xl == 1) & (co == 1)
-    sends_full = (co == 0) | above
-
-    @pl.when((xl == 1) & above)
-    def _():
-        piece().start()
-
-    @pl.when(jnp.logical_not(late) & sends_full)
-    def _():
-        full().start()
-
-    @pl.when(xl == 0)
-    def _():
-        half(0).start()
-        half(1).start()
-
-    def wait_slot(s):
-        copy(own, kbuf.at[s], s_p1.at[0], r_slot.at[s], sibling).wait_recv()
 
     for c in inputs[2:]:
         c.wait()
@@ -271,7 +273,7 @@
     def _():
         crecv[4] = jnp.zeros((2, 144, 512), BF16)
 
-    def second(i, meanwhile=None):
+    def second(i, send, meanwhile=None):
         s = jnp.where(co == 0, (0, 1, 3, 2)[i], (3, 0, 2, 1)[i])
         grad_rope = None
         parts = []
@@ -303,6 +305,7 @@
             gw[...] = part
         else:
             gw[...] += part
+        send()
 
     def core_send(i):
         a = jnp.where(co == 0, (0, 1, 3, 2)[i], (4, 1, 3, 2)[i])
@@ -311,16 +314,9 @@
     def z_send(c):
         return copy(sbuf.at[0, c], zrecv, s_z.at[c], r_z.at[0], dev((z + 7) % 8, xl, c, xh, y))
 
-    def x_send(a):
-        return copy(ysum.at[a, 1 - xh], xrecv.at[a], s_x.at[a], r_x.at[a], dev(z, xl, co, 1 - xh, y))
-
     def y_send(a, t):
         to = (y + t) % 4
-        if a in X_FIRST:
-            src, dst = xsum.at[a, :, lanes(to)], xyrecv.at[a, t - 1]
-        else:
-            src, dst = ysum.at[a, :, :, lanes(to)], yrecv.at[a, t - 1]
-        return copy(src, dst, s_y.at[a, t - 1], r_y.at[a, t - 1], dev(z, xl, co, xh, to))
+        return copy(ysum.at[a, :, :, lanes(to)], yrecv.at[a, t - 1], s_y.at[a, t - 1], r_y.at[a, t - 1], dev(z, xl, co, xh, to))
 
     def finish(a):
         def wait():
@@ -334,30 +330,19 @@
         else:
             wait()
         ysum[a] = (total + crecv[a].astype(F32)).astype(BF16)
-        if a in X_FIRST:
-            x_send(a).start()
-        else:
-            for t in (2, 1, 3):
-                y_send(a, t).start()
-
-    def middle(a):
-        x_send(a).wait_recv()
-        xsum[a] = (ysum[a, xh].astype(F32) + xrecv[a].astype(F32)).astype(BF16)
         for t in (2, 1, 3):
             y_send(a, t).start()
 
     def o_send(a, d):
         owner = (2 * chip + 29 + a) % 32
         to = (xh + d) % 2
-        src = tbuf.at[a, 0] if a in X_FIRST else tbuf.at[a, to]
         k = FIRST_PART[a] + d
-        return copy(src, orecv.at[k, co], s_o.at[a, d], r_o.at[k, co], (owner, to * 4 + y))
+        return copy(tbuf.at[a, to], orecv.at[k, co], s_o.at[a, d], r_o.at[k, co], (owner, to * 4 + y))
 
     def o_each(a, remote, here):
         def both():
             remote(0)
-            if a not in X_FIRST:
-                remote(1)
+            remote(1)
 
         if a < 3:
             pl.when(chip > 0)(both)
@@ -370,19 +355,13 @@
     def stage(a):
         for t in (1, 2, 3):
             y_send(a, t).wait_recv()
-        if a in X_FIRST:
-            total = xsum[a, :, lanes(y)].astype(F32)
-            for t in range(3):
-                total = total + xyrecv[a, t].astype(F32)
-            tbuf[a, 0] = total.astype(BF16)
-        else:
-            total = ysum[a, :, :, lanes(y)].astype(F32)
-            for t in range(3):
-                total = total + yrecv[a, t].astype(F32)
-            tbuf[a] = total.astype(BF16)
+        total = ysum[a, :, :, lanes(y)].astype(F32)
+        for t in range(3):
+            total = total + yrecv[a, t].astype(F32)
+        tbuf[a] = total.astype(BF16)
 
         def here():
-            orecv[FIRST_PART[a], co] = tbuf[a, 0] if a in X_FIRST else tbuf[a, xh]
+            orecv[FIRST_PART[a], co] = tbuf[a, xh]
 
         o_each(a, lambda d: o_send(a, d).start(), here)
 
@@ -403,6 +382,9 @@
         return copy(
             fin, out_ref.at[:, xh, :, lanes(y)], s_ag.at[t - 1], r_ag.at[t - 1], (ctx, (head + t) % 8)
         )
+
+    def mine_out():
+        return pltpu.make_async_copy(fin, out_ref.at[:, xh, :, lanes(y)], s_out.at[2])
 
     def final(count, parts):
         @pl.when(chip < 15)
@@ -418,28 +400,24 @@
         fin[...] = total.astype(BF16)
         for t in (2, 6, 1, 7, 3, 5, 4):
             ag(t).start()
-        out_ref[:, xh, :, lanes(y)] = fin[...]
-
-    second(0)
-
+        mine_out().start()
+
+    def send_first():
+        @pl.when((co == 0) & below)
+        def _():
+            z_send(0).start()
+            z_send(1).start()
+
+        @pl.when(co == 1)
+        def _():
+            core_send(0).start()
+
+    second(0, send_first)
     hear(1)
     tell(2)
-
-    @pl.when((co == 0) & below)
-    def _():
-        z_send(0).start()
-        z_send(1).start()
-
-    @pl.when(co == 1)
-    def _():
-        core_send(0).start()
-
-    second(1)
-    core_send(1).start()
-    second(2, lambda: finish(1))
-    core_send(2).start()
-    second(3, lambda: finish(3))
-    core_send(3).start()
+    second(1, lambda: core_send(1).start())
+    second(2, lambda: core_send(2).start(), lambda: finish(1))
+    second(3, lambda: core_send(3).start(), lambda: finish(3))
     g1().start()
     finish(2)
     g1().wait_recv()
@@ -453,7 +431,6 @@
     hear(2)
     for t in range(1, 8):
         g3(t).start()
-    middle(2)
 
     stage(4)
     stage(2)
@@ -464,19 +441,26 @@
 
     @pl.when(co == 1)
     def _():
-        final(3, ([(0, 0), (0, 1)], [(1, 0), (2, 0), (2, 1)]))
+        final(4, ([(0, 0), (0, 1), (1, 0), (1, 1)], [(2, 0), (3, 0), (3, 1)]))
 
     for h in range(HEADS):
         dq_ref[:, h * 192 : (h + 1) * 192] = (dq_acc[h] * SCALE).astype(BF16)
+    dq_out = pltpu.make_async_copy(dq_ref, dq_hbm, s_out.at[0])
+    dq_out.start()
     for t in range(1, 8):
         g3(t).wait_recv()
     total = g3buf[z].astype(F32)
     for t in range(7):
         total = total + g3recv[t].astype(F32)
     gwo_ref[...] = total
+    gw_out = pltpu.make_async_copy(gwo_ref, gwo_hbm, s_out.at[1])
+    gw_out.start()
     for t in range(1, 8):
         ag(t).wait_recv()
 
+    mine_out().wait()
+    dq_out.wait()
+    gw_out.wait()
     pl.when(sends_full)(lambda: full().wait_send())
     pl.when((xl == 1) & (co == 0) & above)(lambda: piece().wait_send())
 
@@ -512,8 +496,6 @@
     for i in range(1, 4):
         core_send(i).wait_send()
     for a in range(1, 5):
-        if a in X_FIRST:
-            x_send(a).wait_send()
         for t in (1, 2, 3):
             y_send(a, t).wait_send()
         o_each(a, lambda d: o_send(a, d).wait_send(), None)
@@ -550,8 +532,9 @@
             jax.ShapeDtypeStruct((16, 512), F32),
         ),
         in_specs=[hbm] * 5,
-        out_specs=(vm, vm, vm),
+        out_specs=(hbm, hbm, hbm),
         scratch_shapes=[
+            V((ROWS, 384), BF16), V((16, 512), F32), dma((3,)),
             V((4, KEY_ROWS, ROWS), BF16), V((304, 128), BF16), V((2, 144, ROWS), BF16),
             V((ROWS, 384), BF16), V((ROWS, 256), BF16), V((512, 512), BF16), V((8, 128), jnp.int32),
             V((2, ROWS, NOPE + ROPE + MARKS), BF16), V((2, 192, ROWS), BF16), V((2, 128, ROWS), BF16), V((512, 512), BF16),
@@ -559,14 +542,14 @@
             V((2, ROWS, 1), F32), V((2, ROWS, 1), F32), V((2, ROWS, 1), F32), V((4, 2, ROWS, 1), F32),
             V((2, ROWS, 192), F32), V((16, 2, 16, 512), F32),
             V((5, 2, 2, 144, 512), BF16), V((5, 2, 144, 512), BF16), V((5, 2, 144, 512), BF16),
-            V((5, 3, 2, 144, 128), BF16), V((5, 144, 512), BF16), V((5, 144, 512), BF16), V((5, 3, 144, 128), BF16),
+            V((5, 3, 2, 144, 128), BF16),
             V((5, 2, 144, 128), BF16), V((4, 2, 144, 128), BF16), V((2, 144, 128), BF16),
             V((16, 16, 512), F32), V((8, 2, 16, 512), BF16), V((8, 16, 512), BF16), V((8, 16, 512), BF16),
             V((7, 16, 512), BF16),
-            dma((5,)), dma((4,)), dma((8,)), dma((8,)), dma((2,)), dma((4,)), dma((5,)), dma((5, 3)), dma((5, 2)), dma((7,)),
+            dma((5,)), dma((4,)), dma((8,)), dma((8,)), dma((2,)), dma((4,)), dma((5, 3)), dma((5, 2)), dma((7,)),
             dma((9,)),
-            dma((3,)), dma((1,)), pltpu.SemaphoreType.REGULAR((3,)), dma((8,)), dma((2,)), dma((1,)), dma((5,)), dma((5,)), dma((5, 3)), dma((5, 2)), dma((7,)),
-            dma((9,)),
+            dma((3,)), dma((1,)), pltpu.SemaphoreType.REGULAR((3,)), dma((8,)), dma((2,)), dma((1,)),
+            dma((5,)), dma((5, 3)), dma((5, 2)), dma((7,)), dma((9,)),
         ],
         compiler_params=pltpu.CompilerParams(
             collective_id=0, has_side_effects=True, vmem_limit_bytes=58 * 1024 * 1024

time: 61.5 us -> 60.5 us (0.984)
  the two profiles are of different devices: /device:TPU:129 before, /device:TPU:103 now
where the time goes in v4:
time: 60.5 us; the launch traced here: 60.4 us
  Pallas kernels  59.6 us (99%)
  between operations  0.8 us (1%)
    pallas_call x1, Pallas kernels, local(): pl.pallas_call(body, out_shape=(jax.ShapeDtypeStruct((ROWS, HEADS * (NOPE...  57.5 us
    pallas_call x1, Pallas kernels, local(): pl.pallas_call(place, out_shape=(jax.ShapeDtypeStruct((ROWS, HEADS * (NOP...  2.05 us

profile of v4, /device:TPU:103, one launch (start us, length us, event | category | flops | bytes accessed | tf_op | source)
XLA Modules:
  0.0 60.4 jit_solution(7667744682798113075)
XLA Ops:
  0.6 57.5 %shard_map.76 = (bf16[512,384]{1,0:T(8,128)(2,1)}, bf16[2,2,144,512]{3,2,1,0:T(8,128)(2,1)}, f32[16,512]{1,0:T(8,128)}) custom-call(bf16[576,512]{1,0:T(8,128)(2,1)} %bitcast.5, bf16[512,384]{1,0:T(8,128)(2,1)} %q_hbm.1, bf16[512,256]{1,0:T(8,128)(2,1)} %do_hbm.1, bf16[512,512]{1,0:T(8,128)(2,1)} %w_hbm.1, s32[128,128]{1,0:T(8,128)} %bitcast.7), custom_call_target="tpu_custom_call" | custom-call | flops 7000000000 | bytes 4000000 | tf_op jit(solution)/shard_map/pallas_call | solution.py:527
  58.2 2.1 %shard_map.77 = (bf16[512,384]{1,0:T(8,128)(2,1)}, bf16[576,512]{1,0:T(8,128)(2,1)}, f32[16,512]{1,0:T(8,128)}) custom-call(bf16[512,384]{1,0:T(8,128)(2,1)} %get-tuple-element.9.dq, bf16[576,512]{1,0:T(8,128)(2,1)} %bitcast.4, f32[16,512]{1,0:T(8,128)} %get-tuple-element.11.gwo), custom_call_target="tpu_custom_call" | custom-call | tf_op jit(solution)/shard_map/pallas_call | solution.py:559

commit v5 on v4

--- a/solution.py
+++ b/solution.py
@@ -432,8 +432,8 @@
     for t in range(1, 8):
         g3(t).start()
 
+    stage(2)
     stage(4)
-    stage(2)
 
     @pl.when(co == 0)
     def _():

time: 60.5 us -> 59.9 us (0.990)
  the two profiles are of different devices: /device:TPU:103 before, /device:TPU:129 now
where the time goes in v5:
time: 59.9 us; the launch traced here: 59.7 us
  Pallas kernels  58.9 us (98%)
  between operations  0.8 us (1%)
    pallas_call x1, Pallas kernels, local(): pl.pallas_call(body, out_shape=(jax.ShapeDtypeStruct((ROWS, HEADS * (NOPE...  56.9 us
    pallas_call x1, Pallas kernels, local(): pl.pallas_call(place, out_shape=(jax.ShapeDtypeStruct((ROWS, HEADS * (NOP...  2.05 us

profile of v5, /device:TPU:129, one launch (start us, length us, event | category | flops | bytes accessed | tf_op | source)
XLA Modules:
  0.0 59.7 jit_solution(3498061725081004313)
XLA Ops:
  0.6 56.9 %shard_map.76 = (bf16[512,384]{1,0:T(8,128)(2,1)}, bf16[2,2,144,512]{3,2,1,0:T(8,128)(2,1)}, f32[16,512]{1,0:T(8,128)}) custom-call(bf16[576,512]{1,0:T(8,128)(2,1)} %bitcast.5, bf16[512,384]{1,0:T(8,128)(2,1)} %q_hbm.1, bf16[512,256]{1,0:T(8,128)(2,1)} %do_hbm.1, bf16[512,512]{1,0:T(8,128)(2,1)} %w_hbm.1, s32[128,128]{1,0:T(8,128)} %bitcast.7), custom_call_target="tpu_custom_call" | custom-call | flops 7000000000 | bytes 4000000 | tf_op jit(solution)/shard_map/pallas_call | solution.py:527
  57.5 2.1 %shard_map.77 = (bf16[512,384]{1,0:T(8,128)(2,1)}, bf16[576,512]{1,0:T(8,128)(2,1)}, f32[16,512]{1,0:T(8,128)}) custom-call(bf16[512,384]{1,0:T(8,128)(2,1)} %get-tuple-element.9.dq, bf16[576,512]{1,0:T(8,128)(2,1)} %bitcast.4, f32[16,512]{1,0:T(8,128)} %get-tuple-element.11.gwo), custom_call_target="tpu_custom_call" | custom-call | tf_op jit(solution)/shard_map/pallas_call | solution.py:559

commit v6 on v5

--- a/solution.py
+++ b/solution.py
@@ -426,23 +426,23 @@
     stage(1)
     finish(4)
     stage(3)
+
+    stage(2)
+    stage(4)
+
+    @pl.when(co == 0)
+    def _():
+        final(4, ([(0, 0), (0, 1), (1, 0), (1, 1)], [(2, 1), (3, 0), (3, 1)]))
+
+    @pl.when(co == 1)
+    def _():
+        final(4, ([(0, 0), (0, 1), (1, 0), (1, 1)], [(2, 0), (3, 0), (3, 1)]))
+
     g2().wait_recv()
     g3buf[...] = (g2buf[:, xl].astype(F32) + g2recv[...].astype(F32)).astype(BF16)
     hear(2)
     for t in range(1, 8):
         g3(t).start()
-
-    stage(2)
-    stage(4)
-
-    @pl.when(co == 0)
-    def _():
-        final(4, ([(0, 0), (0, 1), (1, 0), (1, 1)], [(2, 1), (3, 0), (3, 1)]))
-
-    @pl.when(co == 1)
-    def _():
-        final(4, ([(0, 0), (0, 1), (1, 0), (1, 1)], [(2, 0), (3, 0), (3, 1)]))
-
     for h in range(HEADS):
         dq_ref[:, h * 192 : (h + 1) * 192] = (dq_acc[h] * SCALE).astype(BF16)
     dq_out = pltpu.make_async_copy(dq_ref, dq_hbm, s_out.at[0])

time: 59.9 us -> 63.8 us (1.065)
  the two profiles are of different devices: /device:TPU:129 before, /device:TPU:1 now
where the time goes in v6:
time: 63.8 us; the launch traced here: 63.7 us
  Pallas kernels  62.9 us (99%)
  between operations  0.8 us (1%)
    pallas_call x1, Pallas kernels, local(): pl.pallas_call(body, out_shape=(jax.ShapeDtypeStruct((ROWS, HEADS * (NOPE...  60.9 us
    pallas_call x1, Pallas kernels, local(): pl.pallas_call(place, out_shape=(jax.ShapeDtypeStruct((ROWS, HEADS * (NOP...  2.05 us

profile of v6, /device:TPU:1, one launch (start us, length us, event | category | flops | bytes accessed | tf_op | source)
XLA Modules:
  0.0 63.7 jit_solution(15623139771372939043)
XLA Ops:
  0.6 60.9 %shard_map.76 = (bf16[512,384]{1,0:T(8,128)(2,1)}, bf16[2,2,144,512]{3,2,1,0:T(8,128)(2,1)}, f32[16,512]{1,0:T(8,128)}) custom-call(bf16[576,512]{1,0:T(8,128)(2,1)} %bitcast.5, bf16[512,384]{1,0:T(8,128)(2,1)} %q_hbm.1, bf16[512,256]{1,0:T(8,128)(2,1)} %do_hbm.1, bf16[512,512]{1,0:T(8,128)(2,1)} %w_hbm.1, s32[128,128]{1,0:T(8,128)} %bitcast.7), custom_call_target="tpu_custom_call" | custom-call | flops 7000000000 | bytes 4000000 | tf_op jit(solution)/shard_map/pallas_call | solution.py:527
  61.5 2.1 %shard_map.77 = (bf16[512,384]{1,0:T(8,128)(2,1)}, bf16[576,512]{1,0:T(8,128)(2,1)}, f32[16,512]{1,0:T(8,128)}) custom-call(bf16[512,384]{1,0:T(8,128)(2,1)} %get-tuple-element.9.dq, bf16[576,512]{1,0:T(8,128)(2,1)} %bitcast.4, f32[16,512]{1,0:T(8,128)} %get-tuple-element.11.gwo), custom_call_target="tpu_custom_call" | custom-call | tf_op jit(solution)/shard_map/pallas_call | solution.py:559
